TPU v7x, 256 devices: a whole 4x4x8 slice. The times are simulated.
256 devices in a mesh: frame: 16 (over y, x), pixel: 16 (over z, core).
Axes of the slice: x: 4, y: 4, z: 8, core: 2. Of those that a mesh axis runs over, the one named last changes fastest.
Arguments:
- tokens: bfloat16 [16, 512, 2048], P('frame', 'pixel'), may hold values from -20 to 20
- spatial_inputs: bfloat16 [16, 512, 6144], P('frame', 'pixel'), may hold values from -6 to 6
- temporal_inputs: bfloat16 [16, 512, 6144], P('frame', 'pixel'), may hold values from -6 to 6
- gate_spatial: float32 [2048], replicated, may hold values from 1 to 4
- gate_temporal: float32 [2048], replicated, may hold values from 1 to 4
- norm_gain: float32 [2048], replicated, may hold values from 0.1 to 1.9
- route_experts: int32 [16, 512, 6], P('frame', 'pixel'), may hold values from 0 to 63, as said below
- route_weights: float32 [16, 512, 6], P('frame', 'pixel'), may hold values from 0.1 to 0.6
- expert_gate_up: bfloat16 [256, 2048, 704], P(('frame', 'pixel')), may hold values from -0.125 to 0.125
- expert_down: bfloat16 [256, 352, 2048], P(('frame', 'pixel')), may hold values from -0.15625 to 0.15625
Outputs:
- attended: bfloat16 [16, 512, 2048], P('frame', 'pixel')
- expert_mix: bfloat16 [16, 512, 2048], P('frame', 'pixel')
Inputs may be any that keep to these rules, and one draw needn't show every extreme that they name: `route_experts`: each row names 6 different experts. Within one frame, each aligned block of 32 positions names any one expert at most 8 times, and in every such block some experts exactly 8 times.
All inputs are finite; a program needn't handle non-finite values.
Results may differ from a plain program's by a relative error of at most 0.02.
Values may be sent and summed in bfloat16 or wider, within the bound.
A program may use at most 64 MiB of HBM per device.

v0:
```python
import math

import jax
import jax.numpy as jnp
from jax import lax
from jax.sharding import PartitionSpec as P

HEADS = 16
HDIM = 128
TOP = 6
EXP_COL = 4
CAP = 8


def attend(queries, key_rows, values):
    divisor = math.sqrt(queries.shape[-1])
    scores = (
        jnp.einsum("bqhd,bkhd->bhqk", queries, key_rows, preferred_element_type=jnp.float32)
        / divisor
    )
    row_max = jnp.max(scores, axis=-1, keepdims=True)
    weights = jnp.exp(scores - row_max)
    row_total = jnp.sum(weights, axis=-1)
    rounded = weights.astype(jnp.bfloat16)
    output = jnp.einsum("bhqk,bkhd->bqhd", rounded, values, preferred_element_type=jnp.float32)
    return (output / jnp.transpose(row_total, (0, 2, 1))[..., None]).astype(jnp.bfloat16)


def pixel_attend(item_block):
    by_pixel = jnp.transpose(item_block, (1, 0, 2, 3, 4))
    output = attend(by_pixel[:, :, 0], by_pixel[:, :, 1], by_pixel[:, :, 2])
    return jnp.transpose(output, (1, 0, 2, 3))


def expert_rows(row_block, gate_up, down_rows):
    layout = row_block.shape
    flat_rows = row_block.reshape(-1, layout[-1])
    hidden_width = down_rows.shape[1]
    gate_and_up = jnp.dot(flat_rows, gate_up[0], preferred_element_type=jnp.float32)
    active = (jax.nn.silu(gate_and_up[:, :hidden_width]) * gate_and_up[:, hidden_width:]).astype(
        jnp.bfloat16
    )
    partial_out = jnp.dot(active, down_rows[0], preferred_element_type=jnp.float32).astype(
        jnp.bfloat16
    )
    return partial_out.reshape(layout)


def slice_work(row_block, gate_up, down_rows):
    return lax.all_to_all(
        expert_rows(row_block, gate_up, down_rows), "frame", split_axis=0, concat_axis=0, tiled=True
    )


def per_device(
    tokens,
    spatial_inputs,
    temporal_inputs,
    gate_spatial,
    gate_temporal,
    norm_gain,
    route_experts,
    route_weights,
    expert_gate_up,
    expert_down,
):
    frames_here, pixels_here, model_width = tokens.shape
    spatial_packed = spatial_inputs.reshape(frames_here, pixels_here, 3, HEADS, HDIM)
    key_rows, value_rows = (
        lax.all_gather(spatial_packed[:, :, 1], "pixel", axis=1, tiled=True),
        lax.all_gather(spatial_packed[:, :, 2], "pixel", axis=1, tiled=True),
    )
    spatial = attend(spatial_packed[:, :, 0], key_rows, value_rows)
    temporal_packed = temporal_inputs.reshape(frames_here, pixels_here, 3, HEADS, HDIM)
    by_frames = pixel_attend(
        lax.all_to_all(temporal_packed, "frame", split_axis=3, concat_axis=0, tiled=True)
    )
    temporal = lax.all_to_all(by_frames, "frame", split_axis=0, concat_axis=2, tiled=True)
    combined = (
        tokens.astype(jnp.float32)
        + gate_spatial * spatial.reshape(frames_here, pixels_here, model_width).astype(jnp.float32)
        + gate_temporal
        * temporal.reshape(frames_here, pixels_here, model_width).astype(jnp.float32)
    )
    attended = combined.astype(jnp.bfloat16)
    widened = attended.astype(jnp.float32)
    mean_square = jnp.mean(widened * widened, axis=-1, keepdims=True)
    expert_input = (
        (widened * lax.rsqrt(mean_square + 1e-06) * norm_gain)
        .astype(jnp.bfloat16)
        .reshape(-1, model_width)
    )
    columns = lax.axis_size("pixel")
    slices = lax.axis_size("frame") // EXP_COL
    experts = columns * EXP_COL
    flat_experts = route_experts.reshape(-1)
    assigned = flat_experts.shape[0]
    one_hot = (flat_experts[:, None] == jnp.arange(experts, dtype=jnp.int32)[None, :]).astype(
        jnp.int32
    )
    slot_rank = jnp.sum(jnp.cumsum(one_hot, axis=0) * one_hot, axis=1) - 1
    slot_index = (flat_experts % EXP_COL * columns + flat_experts // EXP_COL) * CAP + slot_rank
    token_index = jnp.arange(assigned, dtype=jnp.int32) // TOP
    outgoing = (
        jnp.zeros((experts * CAP, model_width), jnp.bfloat16)
        .at[slot_index]
        .set(expert_input[token_index])
    )
    outgoing = outgoing.reshape(EXP_COL, columns, CAP, model_width)
    arrived = lax.all_to_all(outgoing, "pixel", split_axis=1, concat_axis=1, tiled=True)
    copies = jnp.broadcast_to(
        arrived[:, None], (EXP_COL, slices, columns, CAP, model_width)
    ).reshape(EXP_COL * slices, columns, CAP, model_width)
    returned = slice_work(
        lax.all_to_all(copies, "frame", split_axis=0, concat_axis=0, tiled=True),
        expert_gate_up,
        expert_down,
    )
    summed = jnp.sum(
        returned.astype(jnp.float32).reshape(EXP_COL, slices, columns, CAP, model_width), axis=1
    ).astype(jnp.bfloat16)
    results = lax.all_to_all(summed, "pixel", split_axis=1, concat_axis=1, tiled=True).reshape(
        experts * CAP, model_width
    )
    picked = results[slot_index]
    expert_mix = jnp.sum(
        picked.astype(jnp.float32).reshape(-1, TOP, model_width)
        * route_weights.reshape(-1, TOP, 1),
        axis=1,
    )
    expert_mix = expert_mix.astype(jnp.bfloat16).reshape(frames_here, pixels_here, model_width)
    return (attended, expert_mix)


def solution(mesh):
    in_specs = (
        P("frame", "pixel", None),
        P("frame", "pixel", None),
        P("frame", "pixel", None),
        P(),
        P(),
        P(),
        P("frame", "pixel", None),
        P("frame", "pixel", None),
        P(("frame", "pixel"), None, None),
        P(("frame", "pixel"), None, None),
    )
    out_specs = (P("frame", "pixel", None), P("frame", "pixel", None))
    return jax.shard_map(
        per_device, mesh=mesh, in_specs=in_specs, out_specs=out_specs, check_vma=False
    )
```

profile of v0, /device:TPU:1, one launch (start us, length us, event | category | flops | bytes accessed | tf_op | source)
XLA Modules:
  0.0 453.5 jit_solution(1510410869926070589)
XLA Ops:
  7.2 1.2 copy.87
  8.5 0.7 copy.83
  9.2 0.7 copy.84
  10.0 1.1 copy.88
  11.0 0.9 copy.66
  11.9 7.6 %all-to-all-start = ((bf16[1,32,3,16,128]{4,1,2,0,3:T(8,128)(2,1)}), bf16[1,32,3,16,128]{4,1,2,0,3:T(8,128)(2,1)S(1)}, u32[]{:S(2)}, u32[]{:S(2)}) async-start(bf16[1,32,3,16,128]{4,1,2,0,3:T(8,128)(2,1)} %copy.66), calls=%async_computation | async-start | bytes 786432 | tf_op jit(solution)/shard_map/all_to_all | solution.py:76
  19.5 0.1 copy.71
  19.6 0.1 eq.24
  19.7 0.1 reshape.403
  19.8 0.6 reduce-window.6
  20.4 0.2 slice_reduce_fusion
  20.7 0.1 bitcast_bitcast_fusion
  20.8 7.8 %all-to-all-done = bf16[1,32,3,16,128]{4,1,2,0,3:T(8,128)(2,1)S(1)} async-done(((bf16[1,32,3,16,128]{4,1,2,0,3:T(8,128)(2,1)}), bf16[1,32,3,16,128]{4,1,2,0,3:T(8,128)(2,1)S(1)}, u32[]{:S(2)}, u32[]{:S(2)}) %all-to-all-start) | async-done | bytes 393248 | tf_op jit(solution)/shard_map/all_to_all | solution.py:76
  28.6 0.2 copy.104
  28.8 0.2 fusion.51
  29.0 0.1 fusion.40
  29.1 0.3 fusion.26
  29.4 0.7 copy.69
  30.0 3.5 all-to-all-start.1
  33.6 6.8 %all-to-all-done.1 = bf16[16,32,1,128]{3,1,2,0:T(8,128)(2,1)S(1)} async-done(((bf16[16,32,1,128]{3,1,2,0:T(8,128)(2,1)}), bf16[16,32,1,128]{3,1,2,0:T(8,128)(2,1)S(1)}, u32[]{:S(2)}, u32[]{:S(2)}) %all-to-all-start.1) | async-done | bytes 131104 | tf_op jit(solution)/shard_map/all_to_all | solution.py:78
  40.4 0.2 copy.70
  40.6 13.1 %all-gather.5.cloned.1.call-done = bf16[1,512,1,16,128]{4,1,3,2,0:T(8,128)(2,1)} async-done(((bf16[1,32,1,16,128]{4,1,3,2,0:T(8,128)(2,1)}), bf16[1,512,1,16,128]{4,1,3,2,0:T(8,128)(2,1)}) %all-gather.5.cloned.1.call-update) | async-done | bytes 2097168 | tf_op jit(solution)/shard_map/all_gather | solution.py:70
  53.7 2.5 fusion.52
  56.2 1.0 copy-done.2
  57.2 0.4 fusion.29
  57.6 36.8 %all-gather.7.cloned.1.call-done = bf16[1,512,1,16,128]{4,1,3,2,0:T(8,128)(2,1)} async-done(((bf16[1,32,1,16,128]{4,1,3,2,0:T(8,128)(2,1)}), bf16[1,512,1,16,128]{4,1,3,2,0:T(8,128)(2,1)}) %all-gather.7.cloned.1.call-update) | async-done | bytes 2097168 | tf_op jit(solution)/shard_map/all_gather | solution.py:71
  94.4 2.4 fusion.22
  96.8 0.2 copy.64
  97.0 0.2 fusion.34
  97.3 0.1 fusion.43
  97.4 5.9 %scatter_custom_fusion = bf16[512,2048]{1,0:T(8,128)(2,1)} fusion(s32[192]{0:T(256)S(1)} %bitcast.142, bf16[]{:T(256)} %constant.55.clone.1, bf16[32,2048]{1,0:T(8,128)(2,1)S(1)} %fusion.43, s32[1024]{0:T(1024)S(1)} %pad_clamp_fusion.1), kind=kCustom, calls=%fused_computation.25 | custom fusion | bytes 2097154 | tf_op jit(solution)/shard_map/scatter | solution.py:107
  103.3 1.7 copy.75
  105.0 55.1 %all_to_all.47 = bf16[4,16,8,2048]{3,2,0,1:T(8,128)(2,1)S(1)} all-to-all(bf16[4,16,8,2048]{3,2,0,1:T(8,128)(2,1)S(1)} %copy.75), channel_id=1, replica_groups=mesh['frame'=16,'pixel'=16] {'pixel'}, dimensions={1} | all-to-all | bytes 4194304 | tf_op jit(solution)/shard_map/all_to_all | solution.py:110
  160.2 0.1 copy.76
  160.3 1.1 broadcast_in_dim.5
  161.4 102.6 %all_to_all.48 = bf16[16,16,8,2048]{3,2,1,0:T(8,128)(2,1)S(1)} all-to-all(bf16[16,16,8,2048]{3,2,1,0:T(8,128)(2,1)S(1)} %bitcast.126), channel_id=1, replica_groups=mesh['frame'=16,'pixel'=16] {'frame'}, dimensions={0} | all-to-all | bytes 16777216 | tf_op jit(solution)/shard_map/all_to_all | solution.py:115
  264.0 6.3 %fusion.1 = f32[2048,704]{0,1:T(8,128)S(1)} fusion(bf16[2048,2048]{1,0:T(8,128)(2,1)S(1)} %bitcast.128, bf16[1,2048,704]{1,2,0:T(8,128)(2,1)S(1)} %copy-done), kind=kOutput, calls=%fused_computation.7 | convolution fusion | flops 5905580032 | bytes 17039360 | tf_op jit(solution)/shard_map/dot_general | solution.py:39
  270.3 6.9 %convolution_convert_fusion = bf16[2048,2048]{1,0:T(8,128)(2,1)} fusion(f32[2048,704]{0,1:T(8,128)S(1)} %fusion.1, bf16[1,352,2048]{2,1,0:T(8,128)(2,1)S(1)} %copy-done.10), kind=kOutput, calls=%fused_computation.4 | convolution fusion | flops 2961309696 | bytes 15597568 | tf_op jit(solution)/shard_map/dot_general | solution.py:43
  277.2 99.8 %all_to_all.49 = bf16[16,16,8,2048]{3,2,1,0:T(8,128)(2,1)S(1)} all-to-all(bf16[16,16,8,2048]{3,2,1,0:T(8,128)(2,1)} %bitcast.129), channel_id=1, replica_groups=mesh['frame'=16,'pixel'=16] {'frame'}, dimensions={0} | all-to-all | bytes 16777216 | tf_op jit(solution)/shard_map/all_to_all | solution.py:50
  377.0 2.0 bitcast_reduce_fusion
  379.0 1.6 copy.77
  380.6 5.1 %all-to-all-start.5 = ((bf16[4,16,8,2048]{3,2,0,1:T(8,128)(2,1)}), bf16[4,16,8,2048]{3,2,0,1:T(8,128)(2,1)S(1)}, u32[]{:S(2)}, u32[]{:S(2)}) async-start(bf16[4,16,8,2048]{3,2,0,1:T(8,128)(2,1)} %copy.77), calls=%async_computation.5 | async-start | bytes 4194304 | tf_op jit(solution)/shard_map/all_to_all | solution.py:122
  385.7 0.1 copy.81
  385.8 48.9 %all-to-all-done.5 = bf16[4,16,8,2048]{3,2,0,1:T(8,128)(2,1)S(1)} async-done(((bf16[4,16,8,2048]{3,2,0,1:T(8,128)(2,1)}), bf16[4,16,8,2048]{3,2,0,1:T(8,128)(2,1)S(1)}, u32[]{:S(2)}, u32[]{:S(2)}) %all-to-all-start.5) | async-done | bytes 2097184 | tf_op jit(solution)/shard_map/all_to_all | solution.py:122
  434.7 1.6 copy.78
  436.3 4.8 %gather_fusion = bf16[192,2048]{1,0:T(8,128)(2,1)} fusion(bf16[512,2048]{1,0:T(8,128)(2,1)} %bitcast.127, s32[1024]{0:T(1024)S(1)} %pad_clamp_fusion), kind=kCustom, calls=%fused_computation.1 | custom fusion | bytes 1573632 | tf_op jit(solution)/shard_map/gather | solution.py:125
  441.1 2.5 reshape.417
  443.6 3.0 multiply_reduce_fusion
  (39 shorter events, 0.4 us)
Async XLA Ops:
  7.2 256.8 %copy-start = (bf16[1,2048,704]{1,2,0:T(8,128)(2,1)S(1)}, bf16[1,2048,704]{1,2,0:T(8,128)(2,1)}, u32[]{:S(2)}) copy-start(bf16[1,2048,704]{1,2,0:T(8,128)(2,1)} %param.18) | copy-start | bytes 8650756
  7.2 46.5 %all-gather.5.cloned.1.call-start = ((), (), s32[]{:S(2)}) async-start(), calls=%async_computation.6 | async-start | bytes 2228224 | tf_op jit(solution)/shard_map/all_gather | solution.py:70
  8.4 11.0 %copy-start.8 = (s32[1,32,6]{1,0,2:T(1,128)S(1)}, s32[1,32,6]{1,0,2:T(1,128)}, u32[]{:S(2)}) copy-start(s32[1,32,6]{1,0,2:T(1,128)} %param.16) | copy-start | bytes 2308
  9.2 85.2 %all-gather.7.cloned.1.call-start = ((), (), s32[]{:S(2)}) async-start(), calls=%async_computation.7 | async-start | bytes 2228224 | tf_op jit(solution)/shard_map/all_gather | solution.py:71
  11.9 16.8 %all-to-all-start = ((bf16[1,32,3,16,128]{4,1,2,0,3:T(8,128)(2,1)}), bf16[1,32,3,16,128]{4,1,2,0,3:T(8,128)(2,1)S(1)}, u32[]{:S(2)}, u32[]{:S(2)}) async-start(bf16[1,32,3,16,128]{4,1,2,0,3:T(8,128)(2,1)} %copy.66), calls=%async_computation | async-start | bytes 786432 | tf_op jit(solution)/shard_map/all_to_all | solution.py:76
  30.0 10.3 %all-to-all-start.1 = ((bf16[16,32,1,128]{3,1,2,0:T(8,128)(2,1)}), bf16[16,32,1,128]{3,1,2,0:T(8,128)(2,1)S(1)}, u32[]{:S(2)}, u32[]{:S(2)}) async-start(bf16[16,32,1,128]{3,1,2,0:T(8,128)(2,1)} %copy.69), calls=%async_computation.1 | async-start | bytes 262144 | tf_op jit(solution)/shard_map/all_to_all | solution.py:78
  56.2 1.0 copy-start.2
  57.5 39.5 %copy-start.4 = (bf16[1,32,2048]{2,1,0:T(8,128)(2,1)S(1)}, bf16[1,32,2048]{2,1,0:T(8,128)(2,1)}, u32[]{:S(2)}) copy-start(bf16[1,32,2048]{2,1,0:T(8,128)(2,1)} %param.10) | copy-start | bytes 393220
  57.5 39.5 %copy-start.5 = (f32[2048]{0:T(1024)S(1)}, f32[2048]{0:T(1024)}, u32[]{:S(2)}) copy-start(f32[2048]{0:T(1024)} %param.14) | copy-start | bytes 24580
  57.5 39.5 %copy-start.6 = (f32[2048]{0:T(1024)S(1)}, f32[2048]{0:T(1024)}, u32[]{:S(2)}) copy-start(f32[2048]{0:T(1024)} %param.13) | copy-start | bytes 24580
  94.4 2.9 copy-start.7
  97.3 7.8 %copy-start.3 = (bf16[1,32,2048]{2,1,0:T(8,128)(2,1)}, bf16[1,32,2048]{2,1,0:T(8,128)(2,1)S(1)}, u32[]{:S(2)}) copy-start(bf16[1,32,2048]{2,1,0:T(8,128)(2,1)S(1)} %get-tuple-element.3) | copy-start | bytes 393220
  264.0 6.3 %copy-start.10 = (bf16[1,352,2048]{2,1,0:T(8,128)(2,1)S(1)}, bf16[1,352,2048]{2,1,0:T(8,128)(2,1)}, u32[]{:S(2)}) copy-start(bf16[1,352,2048]{2,1,0:T(8,128)(2,1)} %param.19) | copy-start | bytes 4325380
  380.6 5.1 %copy-start.9 = (f32[1,32,6]{1,0,2:T(1,128)S(1)}, f32[1,32,6]{1,0,2:T(1,128)}, u32[]{:S(2)}) copy-start(f32[1,32,6]{1,0,2:T(1,128)} %param.17) | copy-start | bytes 2308
  380.6 54.1 %all-to-all-start.5 = ((bf16[4,16,8,2048]{3,2,0,1:T(8,128)(2,1)}), bf16[4,16,8,2048]{3,2,0,1:T(8,128)(2,1)S(1)}, u32[]{:S(2)}, u32[]{:S(2)}) async-start(bf16[4,16,8,2048]{3,2,0,1:T(8,128)(2,1)} %copy.77), calls=%async_computation.5 | async-start | bytes 4194304 | tf_op jit(solution)/shard_map/all_to_all | solution.py:122
  436.3 10.3 %copy-start.1 = (bf16[1,2048,704]{1,2,0:T(8,128)(2,1)S(1)}, bf16[1,2048,704]{1,2,0:T(8,128)(2,1)}, u32[]{:S(2)}) copy-start(bf16[1,2048,704]{1,2,0:T(8,128)(2,1)} %param.18) | copy-start | bytes 8650756
Sparse Core Ops, SparseCore 0:
  9.9 43.7 all-gather.4
  56.1 38.2 all-gather.6
where the time goes:
time: 454 us; the launch traced here: 453 us
  blocking collectives  258 us (57%)
  waiting for transfers between devices  113 us (25%)
  local copies, waits for them, and re-layouts  26.7 us (6%)
  matrix products  18.5 us (4%)
  starting transfers between devices  16.2 us (4%)
  between operations  14.3 us (3%)
  other arithmetic  6.68 us (1%)
    all_to_all x1, blocking collectives, per_device(): lax.all_to_all(copies, 'frame', split_axis=0, concat_axis=0, tiled=True)  103 us
    all_to_all x1, blocking collectives, slice_work(): lax.all_to_all(expert_rows(row_block, gate_up, down_rows), 'frame', split...  99.8 us
    all_to_all x1, blocking collectives, per_device(): lax.all_to_all(outgoing, 'pixel', split_axis=1, concat_axis=1, tiled=True)  55.1 us
    all_to_all x1, waiting for transfers between devices, per_device(): lax.all_to_all(summed, 'pixel', split_axis=1, concat_axis=1, tiled=True)  48.9 us
    all_gather x1, waiting for transfers between devices, per_device(): lax.all_gather(spatial_packed[:, :, 2], 'pixel', axis=1, tiled=True)  36.8 us
    all_gather x1, waiting for transfers between devices, per_device(): lax.all_gather(spatial_packed[:, :, 1], 'pixel', axis=1, tiled=True)  13.1 us
  transfers between devices with their start and end apart: 5, of which 5 were waited for; matrix products, arithmetic and copies ran while one was open for 2% of the time, Pallas kernels for 0%

commit v1 on v0

v1 whole, which is shorter than its diff:
```python
import math

import jax
import jax.numpy as jnp
from jax import lax
from jax.sharding import PartitionSpec as P

HEADS = 16
HDIM = 128
TOP = 6
CAP = 8
SIDE = 4


def attend(queries, key_rows, values, same=None):
    divisor = math.sqrt(queries.shape[-1])
    scores = jnp.dot(queries, key_rows.T, preferred_element_type=jnp.float32) / divisor
    if same is not None:
        scores = jnp.where(same, scores, -1e30)
    row_max = jnp.max(scores, axis=-1, keepdims=True)
    weights = jnp.exp(scores - row_max)
    row_total = jnp.sum(weights, axis=-1, keepdims=True)
    output = jnp.dot(weights.astype(jnp.bfloat16), values, preferred_element_type=jnp.float32)
    return (output / row_total).astype(jnp.bfloat16)


def per_device(
    tokens,
    spatial_inputs,
    temporal_inputs,
    gate_spatial,
    gate_temporal,
    norm_gain,
    route_experts,
    route_weights,
    expert_gate_up,
    expert_down,
):
    model_width = tokens.shape[-1]
    here = tokens.shape[1]
    frames = lax.axis_size("frame")
    columns = lax.axis_size("pixel")
    ff = expert_down.shape[1]
    half = ff // 2

    def shift(dx):
        return [(f, f // SIDE * SIDE + (f % SIDE + dx) % SIDE) for f in range(frames)]

    gate, up, down = expert_gate_up[0, :, :ff], expert_gate_up[0, :, ff:], expert_down[0]
    piece_a = jnp.concatenate([gate[:, :half], up[:, :half]], axis=1)
    piece_b = jnp.concatenate([gate[:, half:], up[:, half:]], axis=1)
    from_left = lax.ppermute(piece_b, "frame", shift(1))
    from_left_down = lax.ppermute(down[half:], "frame", shift(1))
    from_right = lax.ppermute(piece_a, "frame", shift(-1))
    from_right_down = lax.ppermute(down[:half], "frame", shift(-1))

    routing = jnp.concatenate(
        [route_experts[0].astype(jnp.float32), route_weights[0]], axis=1
    )
    routing = jnp.stack([routing, lax.ppermute(routing, "frame", shift(2))])
    routing = lax.all_gather(routing, "pixel", axis=1, tiled=True)

    spatial_packed = spatial_inputs.reshape(here, 3, HEADS, HDIM)
    spatial_all = lax.all_to_all(spatial_packed, "pixel", split_axis=2, concat_axis=0, tiled=True)
    spatial = attend(spatial_all[:, 0, 0], spatial_all[:, 1, 0], spatial_all[:, 2, 0])
    spatial = lax.all_to_all(spatial, "pixel", split_axis=0, concat_axis=1, tiled=True)

    temporal_packed = temporal_inputs.reshape(here, 3, HEADS, HDIM)
    temporal_all = lax.all_to_all(temporal_packed, "frame", split_axis=2, concat_axis=0, tiled=True)
    place = jnp.arange(here * frames) % here
    temporal = attend(
        temporal_all[:, 0, 0], temporal_all[:, 1, 0], temporal_all[:, 2, 0],
        place[:, None] == place[None, :],
    )
    temporal = lax.all_to_all(temporal, "frame", split_axis=0, concat_axis=1, tiled=True)

    combined = (
        tokens[0].astype(jnp.float32)
        + gate_spatial * spatial.astype(jnp.float32)
        + gate_temporal * temporal.astype(jnp.float32)
    )
    attended = combined.astype(jnp.bfloat16)
    widened = attended.astype(jnp.float32)
    mean_square = jnp.mean(widened * widened, axis=-1, keepdims=True)
    expert_input = (widened * lax.rsqrt(mean_square + 1e-06) * norm_gain).astype(jnp.bfloat16)

    both = jnp.stack([expert_input, lax.ppermute(expert_input, "frame", shift(2))])
    gathered = lax.all_gather(both, "pixel", axis=1, tiled=True)
    gathered = gathered.reshape(2, columns, here, model_width)

    experts = routing[:, :, :TOP].reshape(2, columns, here, 1, TOP)
    weights = routing[:, :, TOP:].reshape(2, columns, here, 1, TOP)
    mine = (
        lax.axis_index("pixel") * SIDE + jnp.arange(SIDE, dtype=jnp.int32)
    ).astype(jnp.float32)
    named = experts == mine[:, None]
    hit = jnp.any(named, axis=-1)
    weight = jnp.sum(jnp.where(named, weights, 0.0), axis=-1)
    rank = jnp.cumsum(hit.astype(jnp.int32), axis=2) - 1
    slots = jnp.arange(CAP, dtype=jnp.int32)
    chosen = hit[..., None] & (rank[..., None] == slots)
    select = chosen.astype(jnp.bfloat16)
    spread = jnp.where(chosen, weight[..., None], 0.0)

    rows = jnp.einsum(
        "fbtjr,fbtd->jfbrd", select, gathered, preferred_element_type=jnp.float32
    ).astype(jnp.bfloat16)
    groups = [[y * SIDE + x for y in range(SIDE)] for x in range(SIDE)]
    arrived = lax.all_to_all(
        rows, "frame", split_axis=0, concat_axis=0, tiled=True, axis_index_groups=groups
    )
    layout = arrived.shape
    flat = arrived.reshape(-1, model_width)

    def partial(gate_up, down_rows):
        width = down_rows.shape[0]
        both_halves = jnp.dot(flat, gate_up, preferred_element_type=jnp.float32)
        active = (jax.nn.silu(both_halves[:, :width]) * both_halves[:, width:]).astype(jnp.bfloat16)
        return jnp.dot(active, down_rows, preferred_element_type=jnp.float32)

    parts = (
        partial(expert_gate_up[0], down)
        + partial(from_left, from_left_down)
        + partial(from_right, from_right_down)
    )
    parts = parts.astype(jnp.bfloat16).reshape(layout)
    returned = lax.all_to_all(
        parts, "frame", split_axis=0, concat_axis=0, tiled=True, axis_index_groups=groups
    )
    mixed = jnp.einsum(
        "fbtjr,jfbrd->fbtd", spread.astype(jnp.bfloat16), returned,
        preferred_element_type=jnp.float32,
    ).astype(jnp.bfloat16).reshape(2, columns * here, model_width)
    mixed = lax.psum_scatter(mixed, "pixel", scatter_dimension=1, tiled=True)
    other = lax.ppermute(mixed[1], "frame", shift(2))
    expert_mix = (mixed[0].astype(jnp.float32) + other.astype(jnp.float32)).astype(jnp.bfloat16)
    return (attended[None], expert_mix[None])


def solution(mesh):
    in_specs = (
        P("frame", "pixel", None),
        P("frame", "pixel", None),
        P("frame", "pixel", None),
        P(),
        P(),
        P(),
        P("frame", "pixel", None),
        P("frame", "pixel", None),
        P(("frame", "pixel"), None, None),
        P(("frame", "pixel"), None, None),
    )
    out_specs = (P("frame", "pixel", None), P("frame", "pixel", None))
    return jax.shard_map(
        per_device, mesh=mesh, in_specs=in_specs, out_specs=out_specs, check_vma=False
    )
```

time: 454 us -> 337 us (0.74)
  blocking collectives: 258 us -> 18.4 us
  waiting for transfers between devices: 113 us -> 197 us
  starting transfers between devices: 16.2 us -> 44 us
  matrix products: 18.5 us -> 34.7 us
  local copies, waits for them, and re-layouts: 26.7 us -> 12.8 us
    all_to_all x3 -> x0, blocking collectives: 258 us -> none  [the longest x1 103 us: per_device(): lax.all_to_all(copies, 'frame', split_axis=0, concat_axis=0, tiled=True)]
    reduce_scatter x0 -> x1, waiting for transfers between devices: none -> 57.5 us  [per_device(): mixed = lax.psum_scatter(mixed, 'pixel', scatter_dimension=1, tiled=True)]
    all_to_all x3 -> x6, waiting for transfers between devices: 63.5 us -> 121 us  [the longest x1 47.3 us: per_device(): lax.all_to_all(parts, 'frame', split_axis=0, concat_axis=0, tiled=True, a...]
    all_gather x2 -> x1, waiting for transfers between devices: 49.9 us -> 8.04 us  [per_device(): gathered = lax.all_gather(both, 'pixel', axis=1, tiled=True)]
    all_to_all x3 -> x6, starting transfers between devices: 16.2 us -> 35 us  [the longest x1 10.3 us: per_device(): lax.all_to_all(spatial_packed, 'pixel', split_axis=2, concat_axis=0, tile...]
    all_gather x0 -> x1, blocking collectives: none -> 18.4 us  [per_device(): routing = lax.all_gather(routing, 'pixel', axis=1, tiled=True)]
    dot_general x6 -> x11, matrix products: 18.5 us -> 31.3 us  [the longest x3 13.7 us: partial(): both_halves = jnp.dot(flat, gate_up, preferred_element_type=jnp.float32)]
    ppermute x0 -> x7, waiting for transfers between devices: none -> 11.3 us  [the longest x1 5.36 us: per_device(): lax.ppermute(expert_input, 'frame', shift(2))]
  transfers between devices with their start and end apart: 5 -> 15, of which waited for: 5 -> 11; matrix products, arithmetic and copies ran while one was open for 2% -> 11% of each run, Pallas kernels for 0% -> 0%
where the time goes in v1:
time: 337 us; the launch traced here: 332 us
  waiting for transfers between devices  197 us (58%)
  starting transfers between devices  44 us (13%)
  matrix products  34.7 us (10%)
  blocking collectives  18.4 us (5%)
  between operations  14.4 us (4%)
  local copies, waits for them, and re-layouts  12.8 us (4%)
  other arithmetic  10.8 us (3%)
    reduce_scatter x1, waiting for transfers between devices, per_device(): mixed = lax.psum_scatter(mixed, 'pixel', scatter_dimension=1, tiled=True)  57.5 us
    all_to_all x1, waiting for transfers between devices, per_device(): lax.all_to_all(parts, 'frame', split_axis=0, concat_axis=0, tiled=True, a...  47.3 us
    all_to_all x1, waiting for transfers between devices, per_device(): lax.all_to_all(rows, 'frame', split_axis=0, concat_axis=0, tiled=True, ax...  38.5 us
    all_gather x1, blocking collectives, per_device(): routing = lax.all_gather(routing, 'pixel', axis=1, tiled=True)  18.4 us
    dot_general x3, matrix products, partial(): both_halves = jnp.dot(flat, gate_up, preferred_element_type=jnp.float32)  13.7 us
    all_to_all x1, waiting for transfers between devices, per_device(): lax.all_to_all(spatial_packed, 'pixel', split_axis=2, concat_axis=0, tile...  13 us
    all_to_all x1, starting transfers between devices, per_device(): lax.all_to_all(spatial_packed, 'pixel', split_axis=2, concat_axis=0, tile...  10.3 us
    dot_general x3, matrix products, partial(): return jnp.dot(active, down_rows, preferred_element_type=jnp.float32)  9.4 us
  transfers between devices with their start and end apart: 15, of which 11 were waited for; matrix products, arithmetic and copies ran while one was open for 11% of the time, Pallas kernels for 0%

profile of v1, /device:TPU:1, one launch (start us, length us, event | category | flops | bytes accessed | tf_op | source)
XLA Modules:
  0.0 332.4 jit_solution(15361218886988540577)
XLA Ops:
  7.2 1.0 copy.117
  8.2 0.9 copy.91
  9.1 7.6 %all-to-all-start.2 = ((bf16[32,3,16,128]{3,0,1,2:T(8,128)(2,1)}), bf16[32,3,16,128]{3,0,1,2:T(8,128)(2,1)S(1)}, u32[]{:S(2)}, u32[]{:S(2)}) async-start(bf16[32,3,16,128]{3,0,1,2:T(8,128)(2,1)} %copy.91), calls=%async_computation.2 | async-start | bytes 786432 | tf_op jit(solution)/shard_map/all_to_all | solution.py:69
  16.7 1.1 copy.116
  17.7 0.8 copy.88
  18.6 7.3 %all-to-all-done.2 = bf16[32,3,16,128]{3,0,1,2:T(8,128)(2,1)S(1)} async-done(((bf16[32,3,16,128]{3,0,1,2:T(8,128)(2,1)}), bf16[32,3,16,128]{3,0,1,2:T(8,128)(2,1)S(1)}, u32[]{:S(2)}, u32[]{:S(2)}) %all-to-all-start.2) | async-done | bytes 393248 | tf_op jit(solution)/shard_map/all_to_all | solution.py:69
  25.8 10.3 %all-to-all-start = ((bf16[32,3,16,128]{3,0,1,2:T(8,128)(2,1)}), bf16[32,3,16,128]{3,0,1,2:T(8,128)(2,1)S(1)}, u32[]{:S(2)}, u32[]{:S(2)}) async-start(bf16[32,3,16,128]{3,0,1,2:T(8,128)(2,1)} %copy.88), calls=%async_computation | async-start | bytes 786432 | tf_op jit(solution)/shard_map/all_to_all | solution.py:64
  36.7 1.0 fusion.9
  37.8 13.0 %all-to-all-done = bf16[32,3,16,128]{3,0,1,2:T(8,128)(2,1)S(1)} async-done(((bf16[32,3,16,128]{3,0,1,2:T(8,128)(2,1)}), bf16[32,3,16,128]{3,0,1,2:T(8,128)(2,1)S(1)}, u32[]{:S(2)}, u32[]{:S(2)}) %all-to-all-start) | async-done | bytes 393248 | tf_op jit(solution)/shard_map/all_to_all | solution.py:64
  50.7 3.5 %all-to-all-start.3 = ((bf16[16,32,128]{2,1,0:T(8,128)(2,1)}), bf16[16,32,128]{2,1,0:T(8,128)(2,1)S(1)}, u32[]{:S(2)}, u32[]{:S(2)}) async-start(bf16[16,32,128]{2,1,0:T(8,128)(2,1)} %bitcast.18), calls=%async_computation.3 | async-start | bytes 262144 | tf_op jit(solution)/shard_map/all_to_all | solution.py:75
  54.8 1.0 fusion.8
  55.9 5.6 %all-to-all-done.3 = bf16[16,32,128]{2,1,0:T(8,128)(2,1)S(1)} async-done(((bf16[16,32,128]{2,1,0:T(8,128)(2,1)}), bf16[16,32,128]{2,1,0:T(8,128)(2,1)S(1)}, u32[]{:S(2)}, u32[]{:S(2)}) %all-to-all-start.3) | async-done | bytes 131104 | tf_op jit(solution)/shard_map/all_to_all | solution.py:75
  61.5 3.7 %all-to-all-start.1 = ((bf16[16,32,128]{2,1,0:T(8,128)(2,1)}), bf16[16,32,128]{2,1,0:T(8,128)(2,1)S(1)}, u32[]{:S(2)}, u32[]{:S(2)}) async-start(bf16[16,32,128]{2,1,0:T(8,128)(2,1)} %bitcast.8), calls=%async_computation.1 | async-start | bytes 262144 | tf_op jit(solution)/shard_map/all_to_all | solution.py:66
  65.5 8.9 %all-to-all-done.1 = bf16[16,32,128]{2,1,0:T(8,128)(2,1)S(1)} async-done(((bf16[16,32,128]{2,1,0:T(8,128)(2,1)}), bf16[16,32,128]{2,1,0:T(8,128)(2,1)S(1)}, u32[]{:S(2)}, u32[]{:S(2)}) %all-to-all-start.1) | async-done | bytes 131104 | tf_op jit(solution)/shard_map/all_to_all | solution.py:66
  74.9 0.9 collective-permute-start.1
  75.8 0.7 multiply_convert_fusion
  76.5 5.4 %collective-permute-done.1 = bf16[32,2048]{1,0:T(8,128)(2,1)S(1)} collective-permute-done((bf16[32,2048]{1,0:T(8,128)(2,1)S(1)}, bf16[32,2048]{1,0:T(8,128)(2,1)S(1)}, u32[]{:S(2)}, u32[]{:S(2)}) %collective-permute-start.1) | collective-permute-done | bytes 131104 | tf_op jit(solution)/shard_map/ppermute | solution.py:87
  81.9 0.7 pad_maximum_fusion.2
  82.9 0.8 collective-permute-start
  83.8 3.3 collective-permute-done
  87.1 18.4 %all_gather.6 = f32[2,512,12]{2,0,1:T(2,128)S(1)} all-gather(f32[2,32,12]{2,0,1:T(2,128)S(1)} %pad_maximum_fusion.3), channel_id=1, replica_groups=mesh['frame'=16,'pixel'=16] {'pixel'}, dimensions={1}, use_global_device_ids=true | all-gather | bytes 52224 | tf_op jit(solution)/shard_map/all_gather | solution.py:61
  105.5 0.6 fusion.58
  106.9 4.1 %reduce-window_add_fusion = s32[2,16,32,4]{3,1,2,0:T(8,128)S(1)} fusion(s32[2,16,32,4]{3,1,2,0:T(8,128)S(1)} %copy.100), kind=kOutput, calls=%fused_computation.28 | output fusion | flops 131072 | bytes 32768 | tf_op jit(solution)/shard_map/jit(cumsum)/reduce_window_sum | solution.py:99
  111.3 8.0 %all-gather.2.cloned.1.call-done = bf16[2,512,2048]{2,1,0:T(8,128)(2,1)} async-done(((bf16[2,32,2048]{2,1,0:T(8,128)(2,1)}), bf16[2,512,2048]{2,1,0:T(8,128)(2,1)}) %all-gather.2.cloned.1.call-update) | async-done | bytes 4194320 | tf_op jit(solution)/shard_map/all_gather | solution.py:88
  119.3 3.4 %fusion.1 = bf16[4,2,16,8,2048]{4,3,0,2,1:T(8,128)(2,1)S(1)} fusion(bf16[2,16,32,2048]{3,2,1,0:T(8,128)(2,1)} %bitcast.133, s32[2,16,32,4]{2,3,1,0:T(4,128)S(1)} %copy.101, pred[2,16,32,4]{2,3,1,0:T(4,128)(4,1)S(1)} %copy.99), kind=kOutput, calls=%fused_computation.4 | convolution fusion | flops 136380416 | bytes 8409088
  122.8 2.3 copy.107
  125.1 4.8 %all-to-all-start.4 = ((bf16[4,2,16,8,2048]{4,3,2,1,0:T(8,128)(2,1)}), bf16[4,2,16,8,2048]{4,3,2,1,0:T(8,128)(2,1)}, u32[]{:S(2)}, u32[]{:S(2)}) async-start(bf16[4,2,16,8,2048]{4,3,2,1,0:T(8,128)(2,1)} %copy.107), calls=%async_computation.4 | async-start | bytes 8388608 | tf_op jit(solution)/shard_map/all_to_all | solution.py:109
  129.9 2.7 slice_bitcast_fusion.2
  132.7 1.8 collective-permute-start.5
  135.0 1.3 pad_maximum_fusion
  136.3 0.5 collective-permute-start.2
  136.8 1.2 pad_maximum_fusion.1
  138.0 2.2 collective-permute-start.4
  140.2 38.5 %all-to-all-done.4 = bf16[4,2,16,8,2048]{4,3,2,1,0:T(8,128)(2,1)} async-done(((bf16[4,2,16,8,2048]{4,3,2,1,0:T(8,128)(2,1)}), bf16[4,2,16,8,2048]{4,3,2,1,0:T(8,128)(2,1)}, u32[]{:S(2)}, u32[]{:S(2)}) %all-to-all-start.4) | async-done | bytes 4194336 | tf_op jit(solution)/shard_map/all_to_all | solution.py:109
  178.7 5.1 %fusion.2 = f32[1024,704]{0,1:T(8,128)S(1)} fusion(bf16[1024,2048]{1,0:T(8,128)(2,1)} %bitcast.33, bf16[1,2048,704]{1,2,0:T(8,128)(2,1)S(1)} %copy-done), kind=kOutput, calls=%fused_computation.5 | convolution fusion | flops 2952790016 | bytes 9961472 | tf_op jit(solution)/shard_map/dot_general | solution.py:117
  183.8 2.4 fusion.5
  186.2 4.3 %fusion.61 = f32[1024,352]{0,1:T(8,128)S(1)} fusion(bf16[1024,2048]{1,0:T(8,128)(2,1)} %bitcast.33, bf16[2048,352]{0,1:T(8,128)(2,1)} %collective-permute-done.2), kind=kOutput, calls=%fused_computation.104 | convolution fusion | flops 1476395008 | bytes 7077888 | tf_op jit(solution)/shard_map/dot_general | solution.py:117
  190.6 2.4 fusion.26
  193.0 4.3 %fusion.62 = f32[1024,352]{0,1:T(8,128)S(1)} fusion(bf16[1024,2048]{1,0:T(8,128)(2,1)} %bitcast.33, bf16[2048,352]{0,1:T(8,128)(2,1)} %collective-permute-done.4), kind=kOutput, calls=%fused_computation.105 | convolution fusion | flops 1476395008 | bytes 7077888 | tf_op jit(solution)/shard_map/dot_general | solution.py:117
  197.3 4.5 %add_convert_fusion = bf16[1024,2048]{1,0:T(8,128)(2,1)} fusion(f32[1024,2048]{1,0:T(8,128)S(1)} %fusion.5, f32[1024,2048]{1,0:T(8,128)S(1)} %fusion.26, bf16[176,2048]{1,0:T(8,128)(2,1)} %collective-permute-done.5, f32[1024,352]{0,1:T(8,128)S(1)} %fusion.62), kind=kOutput, calls=%fused_computation.2 | convolution fusion | flops 745570304 | bytes 23134208 | tf_op jit(solution)/shard_map/dot_general | solution.py:119
  201.9 5.0 %all-to-all-start.5 = ((bf16[4,2,16,8,2048]{4,3,2,1,0:T(8,128)(2,1)}), bf16[4,2,16,8,2048]{4,3,2,1,0:T(8,128)(2,1)}, u32[]{:S(2)}, u32[]{:S(2)}) async-start(bf16[4,2,16,8,2048]{4,3,2,1,0:T(8,128)(2,1)} %bitcast.132), calls=%async_computation.5 | async-start | bytes 8388608 | tf_op jit(solution)/shard_map/all_to_all | solution.py:127
  207.4 47.3 %all-to-all-done.5 = bf16[4,2,16,8,2048]{4,3,2,1,0:T(8,128)(2,1)} async-done(((bf16[4,2,16,8,2048]{4,3,2,1,0:T(8,128)(2,1)}), bf16[4,2,16,8,2048]{4,3,2,1,0:T(8,128)(2,1)}, u32[]{:S(2)}, u32[]{:S(2)}) %all-to-all-start.5) | async-done | bytes 4194336 | tf_op jit(solution)/shard_map/all_to_all | solution.py:127
  254.7 5.5 %bitcast_convert_fusion = bf16[2,16,32,2048]{3,2,1,0:T(8,128)(2,1)} fusion(bf16[4,2,16,8,2048]{4,3,2,1,0:T(8,128)(2,1)} %all-to-all-done.5, bf16[2,16,32,4]{2,3,1,0:T(4,128)(2,1)S(1)} %copy.104, s32[2,16,32,4]{2,3,1,0:T(4,128)S(1)} %copy-done.3, pred[2,16,32,4]{2,3,1,0:T(4,128)(4,1)S(1)} %copy.99), kind=kOutput, calls=%fused_computation | convolution fusion | flops 136413184 | bytes 8417280 | tf_op jit(solution)/shard_map/fbtjr,jfbrd->fbtd/dot_general | solution.py:130
  260.2 57.5 %reduce-scatter.2.cloned.1.call-done = bf16[2,32,2048]{2,1,0:T(8,128)(2,1)} async-done(((bf16[2,512,2048]{2,1,0:T(8,128)(2,1)}), bf16[2,32,2048]{2,1,0:T(8,128)(2,1)}) %reduce-scatter.2.cloned.1.call-update) | async-done | bytes 262160 | tf_op jit(solution)/shard_map/reduce_scatter | solution.py:134
  317.6 0.9 slice_bitcast_fusion.4
  318.6 2.8 collective-permute-start.6
  321.3 2.6 collective-permute-done.6
  324.0 1.6 fusion.46
  (62 shorter events, 4.3 us)
Async XLA Ops:
  9.1 16.8 %all-to-all-start.2 = ((bf16[32,3,16,128]{3,0,1,2:T(8,128)(2,1)}), bf16[32,3,16,128]{3,0,1,2:T(8,128)(2,1)S(1)}, u32[]{:S(2)}, u32[]{:S(2)}) async-start(bf16[32,3,16,128]{3,0,1,2:T(8,128)(2,1)} %copy.91), calls=%async_computation.2 | async-start | bytes 786432 | tf_op jit(solution)/shard_map/all_to_all | solution.py:69
  25.8 24.9 %all-to-all-start = ((bf16[32,3,16,128]{3,0,1,2:T(8,128)(2,1)}), bf16[32,3,16,128]{3,0,1,2:T(8,128)(2,1)S(1)}, u32[]{:S(2)}, u32[]{:S(2)}) async-start(bf16[32,3,16,128]{3,0,1,2:T(8,128)(2,1)} %copy.88), calls=%async_computation | async-start | bytes 786432 | tf_op jit(solution)/shard_map/all_to_all | solution.py:64
  50.7 10.7 %all-to-all-start.3 = ((bf16[16,32,128]{2,1,0:T(8,128)(2,1)}), bf16[16,32,128]{2,1,0:T(8,128)(2,1)S(1)}, u32[]{:S(2)}, u32[]{:S(2)}) async-start(bf16[16,32,128]{2,1,0:T(8,128)(2,1)} %bitcast.18), calls=%async_computation.3 | async-start | bytes 262144 | tf_op jit(solution)/shard_map/all_to_all | solution.py:75
  54.8 19.8 %copy-start.4 = (bf16[1,32,2048]{2,1,0:T(8,128)(2,1)S(1)}, bf16[1,32,2048]{2,1,0:T(8,128)(2,1)}, u32[]{:S(2)}) copy-start(bf16[1,32,2048]{2,1,0:T(8,128)(2,1)} %param.10) | copy-start | bytes 393220
  54.8 19.8 %copy-start.5 = (f32[2048]{0:T(1024)S(1)}, f32[2048]{0:T(1024)}, u32[]{:S(2)}) copy-start(f32[2048]{0:T(1024)} %param.14) | copy-start | bytes 24580
  54.8 19.8 %copy-start.6 = (f32[2048]{0:T(1024)S(1)}, f32[2048]{0:T(1024)}, u32[]{:S(2)}) copy-start(f32[2048]{0:T(1024)} %param.13) | copy-start | bytes 24580
  54.8 20.0 %copy-start.7 = (f32[2048]{0:T(1024)S(1)}, f32[2048]{0:T(1024)}, u32[]{:S(2)}) copy-start(f32[2048]{0:T(1024)} %param.15) | copy-start | bytes 24580
  61.5 12.9 %all-to-all-start.1 = ((bf16[16,32,128]{2,1,0:T(8,128)(2,1)}), bf16[16,32,128]{2,1,0:T(8,128)(2,1)S(1)}, u32[]{:S(2)}, u32[]{:S(2)}) async-start(bf16[16,32,128]{2,1,0:T(8,128)(2,1)} %bitcast.8), calls=%async_computation.1 | async-start | bytes 262144 | tf_op jit(solution)/shard_map/all_to_all | solution.py:66
  65.1 54.2 %all-gather.2.cloned.1.call-start = ((), (), s32[]{:S(2)}) async-start(), calls=%async_computation.7 | async-start | bytes 4456448 | tf_op jit(solution)/shard_map/all_gather | solution.py:88
  65.2 17.4 %copy-start.8 = (s32[1,32,6]{1,0,2:T(1,128)S(1)}, s32[1,32,6]{1,0,2:T(1,128)}, u32[]{:S(2)}) copy-start(s32[1,32,6]{1,0,2:T(1,128)} %param.16) | copy-start | bytes 2308
  65.3 17.5 %copy-start.9 = (f32[1,32,6]{1,0,2:T(1,128)S(1)}, f32[1,32,6]{1,0,2:T(1,128)}, u32[]{:S(2)}) copy-start(f32[1,32,6]{1,0,2:T(1,128)} %param.17) | copy-start | bytes 2308
  74.9 6.9 %collective-permute-start.1 = (bf16[32,2048]{1,0:T(8,128)(2,1)S(1)}, bf16[32,2048]{1,0:T(8,128)(2,1)S(1)}, u32[]{:S(2)}, u32[]{:S(2)}) collective-permute-start(bf16[32,2048]{1,0:T(8,128)(2,1)S(1)} %fusion.38), channel_id=1, source_target_pairs={{0,32},{16,48},{32,0},{48,16},{64,96},{80,112},{96,64},{112,80},{1... | collective-permute-start | bytes 393224 | tf_op jit(solution)/shard_map/ppermute | solution.py:87
  82.9 4.1 %collective-permute-start = (f32[32,12]{1,0:T(8,128)S(1)}, f32[32,12]{1,0:T(8,128)S(1)}, u32[]{:S(2)}, u32[]{:S(2)}) collective-permute-start(f32[32,12]{1,0:T(8,128)S(1)} %pad_maximum_fusion.4), channel_id=1, source_target_pairs={{0,32},{16,48},{32,0},{48,16},{64,96},{80,112},{96,64},{112,80},{1... | collective-permute-start | bytes 4616 | tf_op jit(solution)/shard_map/ppermute | solution.py:60
  111.3 11.5 %copy-start.2 = (s32[2,16,32,4]{2,3,1,0:T(4,128)}, s32[2,16,32,4]{2,3,1,0:T(4,128)S(1)}, u32[]{:S(2)}) copy-start(s32[2,16,32,4]{2,3,1,0:T(4,128)S(1)} %copy.101) | copy-start | bytes 49156
  125.1 53.6 %all-to-all-start.4 = ((bf16[4,2,16,8,2048]{4,3,2,1,0:T(8,128)(2,1)}), bf16[4,2,16,8,2048]{4,3,2,1,0:T(8,128)(2,1)}, u32[]{:S(2)}, u32[]{:S(2)}) async-start(bf16[4,2,16,8,2048]{4,3,2,1,0:T(8,128)(2,1)} %copy.107), calls=%async_computation.4 | async-start | bytes 8388608 | tf_op jit(solution)/shard_map/all_to_all | solution.py:109
  129.9 4.6 %copy-start = (bf16[1,2048,704]{1,2,0:T(8,128)(2,1)S(1)}, bf16[1,2048,704]{1,2,0:T(8,128)(2,1)}, u32[]{:S(2)}) copy-start(bf16[1,2048,704]{1,2,0:T(8,128)(2,1)} %param.18) | copy-start | bytes 8650756
  132.7 64.6 %collective-permute-start.5 = (bf16[176,2048]{1,0:T(8,128)(2,1)}, bf16[176,2048]{1,0:T(8,128)(2,1)}, u32[]{:S(2)}, u32[]{:S(2)}) collective-permute-start(bf16[176,2048]{1,0:T(8,128)(2,1)} %get-tuple-element.12), channel_id=1, source_target_pairs={{0,48},{16,0},{32,16},{48,32},{64,112},{80,64},{96,80},{112,96},{1... | collective-permute-start | bytes 2162696 | tf_op jit(solution)/shard_map/ppermute | solution.py:55
  134.5 56.0 %collective-permute-start.3 = (bf16[176,2048]{1,0:T(8,128)(2,1)}, bf16[176,2048]{1,0:T(8,128)(2,1)}, u32[]{:S(2)}, u32[]{:S(2)}) collective-permute-start(bf16[176,2048]{1,0:T(8,128)(2,1)} %get-tuple-element.13), channel_id=1, source_target_pairs={{0,16},{16,32},{32,48},{48,0},{64,80},{80,96},{96,112},{112,64},{1... | collective-permute-start | bytes 2162696 | tf_op jit(solution)/shard_map/ppermute | solution.py:53
  136.3 49.9 %collective-permute-start.2 = (bf16[2048,352]{0,1:T(8,128)(2,1)}, bf16[2048,352]{0,1:T(8,128)(2,1)}, u32[]{:S(2)}, u32[]{:S(2)}) collective-permute-start(bf16[2048,352]{0,1:T(8,128)(2,1)} %pad_maximum_fusion), channel_id=1, source_target_pairs={{0,16},{16,32},{32,48},{48,0},{64,80},{80,96},{96,112},{112,64},{1... | collective-permute-start | bytes 4325384 | tf_op jit(solution)/shard_map/ppermute | solution.py:52
  138.0 55.0 %collective-permute-start.4 = (bf16[2048,352]{0,1:T(8,128)(2,1)}, bf16[2048,352]{0,1:T(8,128)(2,1)}, u32[]{:S(2)}, u32[]{:S(2)}) collective-permute-start(bf16[2048,352]{0,1:T(8,128)(2,1)} %pad_maximum_fusion.1), channel_id=1, source_target_pairs={{0,48},{16,0},{32,16},{48,32},{64,112},{80,64},{96,80},{112,96},{1... | collective-permute-start | bytes 4325384 | tf_op jit(solution)/shard_map/ppermute | solution.py:54
  178.7 5.1 %copy-start.1 = (bf16[1,352,2048]{2,1,0:T(8,128)(2,1)S(1)}, bf16[1,352,2048]{2,1,0:T(8,128)(2,1)}, u32[]{:S(2)}) copy-start(bf16[1,352,2048]{2,1,0:T(8,128)(2,1)} %param.19) | copy-start | bytes 4325380
  201.9 52.8 %copy-start.3 = (s32[2,16,32,4]{2,3,1,0:T(4,128)S(1)}, s32[2,16,32,4]{2,3,1,0:T(4,128)}, u32[]{:S(2)}) copy-start(s32[2,16,32,4]{2,3,1,0:T(4,128)} %copy-done.2) | copy-start | bytes 49156
  201.9 52.8 %all-to-all-start.5 = ((bf16[4,2,16,8,2048]{4,3,2,1,0:T(8,128)(2,1)}), bf16[4,2,16,8,2048]{4,3,2,1,0:T(8,128)(2,1)}, u32[]{:S(2)}, u32[]{:S(2)}) async-start(bf16[4,2,16,8,2048]{4,3,2,1,0:T(8,128)(2,1)} %bitcast.132), calls=%async_computation.5 | async-start | bytes 8388608 | tf_op jit(solution)/shard_map/all_to_all | solution.py:127
  206.9 110.8 %reduce-scatter.2.cloned.1.call-start = ((), (), s32[]{:S(2)}) async-start(), calls=%async_computation.8 | async-start | bytes 4456448 | tf_op jit(solution)/shard_map/reduce_scatter | solution.py:134
  318.6 5.4 %collective-permute-start.6 = (bf16[32,2048]{1,0:T(8,128)(2,1)S(1)}, bf16[32,2048]{1,0:T(8,128)(2,1)S(1)}, u32[]{:S(2)}, u32[]{:S(2)}) collective-permute-start(bf16[32,2048]{1,0:T(8,128)(2,1)S(1)} %slice_bitcast_fusion.4), channel_id=1, source_target_pairs={{0,32},{16,48},{32,0},{48,16},{64,96},{80,112},{96,64},{112,80},{1... | collective-permute-start | bytes 393224 | tf_op jit(solution)/shard_map/ppermute | solution.py:135
Sparse Core Ops, SparseCore 0:
  82.8 36.5 all-gather.1
  260.3 57.3 reduce-scatter.1

commit v2 on v1

v2 whole, which is shorter than its diff:
```python
import math

import jax
import jax.numpy as jnp
from jax import lax
from jax.experimental import pallas as pl
from jax.experimental.pallas import tpu as pltpu
from jax.sharding import PartitionSpec as P

BF16, F32 = jnp.bfloat16, jnp.float32
D = 2048
HEADS = 16
HDIM = 128
TOP = 6
CAP = 8
SIDE = 4
DEPTH = 8
HERE = 32
FF = 352
HALF = FF // 2
FF_PAD = 384
GROUP = 8 * HERE
SLOTS = GROUP // HERE * CAP
CHUNK = 512


def dot(a, b, dims=(1, 0)):
    return lax.dot_general(
        a, b, (((dims[0],), (dims[1],)), ((), ())), preferred_element_type=F32
    )


def iota(shape, axis):
    return lax.broadcasted_iota(jnp.int32, shape, axis)


def send(src, dst, send_sem, recv_sem, **where):
    pltpu.make_async_remote_copy(
        src_ref=src,
        dst_ref=dst,
        send_sem=send_sem,
        recv_sem=recv_sem,
        device_id=where,
        device_id_type=pl.DeviceIdType.MESH,
    ).start()


def wait_for(ref, sem):
    pltpu.make_async_copy(ref, ref, sem).wait()


def loop(low, high, body):
    def step(i, carry):
        body(i)
        return carry

    lax.fori_loop(low, high, step, 0)


def attend(packed, out, masked):
    def rows(i):
        queries = packed[0, pl.ds(4 * i, 4)].reshape(4 * HERE, HDIM)
        key_rows = packed[1].reshape(HEADS * HERE, HDIM)
        values = packed[2].reshape(HEADS * HERE, HDIM)
        scores = dot(queries, key_rows, (1, 1)) * (1.0 / math.sqrt(HDIM))
        if masked:
            same = iota(scores.shape, 0) % HERE == iota(scores.shape, 1) % HERE
            scores = jnp.where(same, scores, -1e30)
        weights = jnp.exp(scores - jnp.max(scores, axis=-1, keepdims=True))
        total = jnp.sum(weights, axis=-1, keepdims=True)
        result = dot(weights.astype(BF16), values) / total
        out[pl.ds(4 * i, 4)] = result.astype(BF16).reshape(4, HERE, HDIM)

    loop(0, 4, rows)


def kernel(
    tokens, spatial, temporal, gate_s, gate_t, gain, experts, weights, gate_up, down,
    attended_out, mix_out,
    own_gu, own_al, piece_a, piece_b, left_gu, right_gu, own_dn, left_dn, right_dn,
    s_out, s_in, t_out, t_in, s_part, t_part, s_ret, t_ret,
    r_out, r_in, rt, tok, sel, spr, rows_out, arrive, parts, back, mixed, sib, zred, zin,
    fin_out, fin_in,
    load_sem, w_send, w_recv, a_send, a_recv, r_send, r_recv, pair_send, pair_recv,
    z_send, z_recv, c_send, c_recv, y_send, y_recv, b_send, b_recv, m_send, m_recv,
    q_send, q_recv,
):
    f = lax.axis_index("frame")
    p = lax.axis_index("pixel")
    y, x = f // SIDE, f % SIDE
    z, c = p // 2, p % 2
    spot = z % 4

    def at_x(step):
        return y * SIDE + (x + step) % SIDE

    def at_y(other):
        return other * SIDE + x

    load_gu = pltpu.make_async_copy(gate_up, own_gu, load_sem.at[0])
    load_dn = pltpu.make_async_copy(down, own_dn.at[pl.ds(0, FF)], load_sem.at[1])
    load_gu.start()
    load_dn.start()

    barrier = pltpu.get_barrier_semaphore()

    def greet(i):
        pl.semaphore_signal(
            barrier, inc=1, device_id={"pixel": (p + i) % 16}, device_id_type=pl.DeviceIdType.MESH
        )
        pl.semaphore_signal(
            barrier, inc=1, device_id={"frame": (f + i) % 16}, device_id_type=pl.DeviceIdType.MESH
        )

    loop(1, 16, greet)

    for w in range(3):
        for h in range(HEADS):
            at = (w * HEADS + h) * HDIM
            s_out[w, h] = spatial[:, at : at + HDIM]
            t_out[w, h] = temporal[:, at : at + HDIM]
    place = (iota((HERE, 128), 1) == iota((HERE, 128), 0) + spot * HERE).astype(F32)
    exact = dict(precision=lax.Precision.HIGHEST, preferred_element_type=F32)
    over = (((0,), (0,)), ((), ()))
    r_out[...] = jnp.zeros_like(r_out)
    r_out[0:TOP] = lax.dot_general(experts[...].astype(F32), place, over, **exact)
    r_out[8 : 8 + TOP] = lax.dot_general(weights[...], place, over, **exact)

    pl.semaphore_wait(barrier, 30)

    def scatter_heads(i):
        to_f, to_p = (f + i) % 16, (p + i) % 16
        send(t_out.at[:, to_f], t_in.at[:, f], a_send.at[1], a_recv.at[1], frame=to_f)
        send(s_out.at[:, to_p], s_in.at[:, p], a_send.at[0], a_recv.at[0], pixel=to_p)

    loop(1, 16, scatter_heads)

    def scatter_routes(i):
        send(r_out, r_in.at[p], r_send.at[0], r_recv.at[0], pixel=(p + i) % 16)

    loop(1, 16, scatter_routes)
    s_in[:, p] = s_out[:, p]
    t_in[:, f] = t_out[:, f]
    r_in[p] = r_out[...]

    load_gu.wait()
    load_dn.wait()
    own_dn[FF:FF_PAD] = jnp.zeros((FF_PAD - FF, D), BF16)
    src, dst = iota((2 * FF, FF), 0), iota((2 * FF, FF), 1)
    pick_a = (src == jnp.where(dst < HALF, dst, dst + HALF)).astype(BF16)
    pick_b = (src == jnp.where(dst < HALF, dst + HALF, dst + 2 * HALF)).astype(BF16)
    src, dst = iota((2 * FF, 2 * FF_PAD), 0), iota((2 * FF, 2 * FF_PAD), 1)
    pick_al = (
        ((dst < FF) & (src == dst)) | ((dst >= FF_PAD) & (src == dst - FF_PAD + FF))
    ).astype(BF16)

    def cut(i):
        rows = pl.ds(i * 256, 256)
        block = own_gu[rows]
        piece_a[rows] = dot(block, pick_a).astype(BF16)
        piece_b[rows] = dot(block, pick_b).astype(BF16)

    loop(0, 8, cut)
    send(piece_a, right_gu, w_send.at[0], w_recv.at[0], frame=at_x(3))
    send(piece_b, left_gu, w_send.at[1], w_recv.at[1], frame=at_x(1))
    send(own_dn.at[pl.ds(0, HALF)], right_dn, w_send.at[2], w_recv.at[2], frame=at_x(3))
    send(own_dn.at[pl.ds(HALF, HALF)], left_dn, w_send.at[3], w_recv.at[3], frame=at_x(1))

    wait_for(t_in.at[:, pl.ds(0, 15)], a_recv.at[1])
    attend(t_in, t_part, True)

    def return_t(i):
        to = (f + i) % 16
        send(
            t_part.at[to], t_ret.at[:, pl.ds(pl.multiple_of(f * HDIM, HDIM), HDIM)],
            a_send.at[3], a_recv.at[3], frame=to,
        )

    loop(1, 16, return_t)
    t_ret[:, pl.ds(pl.multiple_of(f * HDIM, HDIM), HDIM)] = t_part[f]

    wait_for(s_in.at[:, pl.ds(0, 15)], a_recv.at[0])
    attend(s_in, s_part, False)

    def return_s(i):
        to = (p + i) % 16
        send(
            s_part.at[to], s_ret.at[:, pl.ds(pl.multiple_of(p * HDIM, HDIM), HDIM)],
            a_send.at[2], a_recv.at[2], pixel=to,
        )

    loop(1, 16, return_s)
    s_ret[:, pl.ds(pl.multiple_of(p * HDIM, HDIM), HDIM)] = s_part[p]

    wait_for(r_in.at[pl.ds(0, 15)], r_recv.at[0])
    for g in range(2):
        for core in range(2):
            total = None
            for q in range(4):
                block = r_in[(z + 7 + 4 * g + q) % DEPTH * 2 + core]
                total = block if total is None else total + block
            rt[0, g, core] = total
    send(rt.at[0], rt.at[1], r_send.at[1], r_recv.at[1], frame=at_x(2))

    def align(i):
        rows = pl.ds(i * 256, 256)
        own_al[rows] = dot(own_gu[rows], pick_al).astype(BF16)

    loop(0, 8, align)

    wait_for(t_ret.at[:, pl.ds(0, 15 * HDIM)], a_recv.at[3])
    wait_for(s_ret.at[:, pl.ds(0, 15 * HDIM)], a_recv.at[2])
    attended = (
        tokens[...].astype(F32)
        + gate_s[...] * s_ret[...].astype(F32)
        + gate_t[...] * t_ret[...].astype(F32)
    ).astype(BF16)
    attended_out[...] = attended
    widened = attended.astype(F32)
    mean_square = jnp.mean(widened * widened, axis=-1, keepdims=True)
    tok[0, 0, c, spot] = (widened * lax.rsqrt(mean_square + 1e-06) * gain[...]).astype(BF16)

    mine, other = tok.at[0, 0, c, spot], tok.at[1, 0, c, spot]
    send(mine, other, pair_send.at[0], pair_recv.at[0], frame=at_x(2))

    def spread_rows(frame, step):
        to = (z + step) % DEPTH
        group = (((DEPTH - step) + 1) % DEPTH) // 4
        send(
            tok.at[frame, 0, c, spot], tok.at[frame, group, c, spot],
            z_send.at[frame, step], z_recv.at[frame, group], pixel=to * 2 + c,
        )

    for step in (1, 7, 6):
        spread_rows(0, step)
    wait_for(other, pair_recv.at[0])
    for step in (1, 7, 6):
        spread_rows(1, step)
    for frame in range(2):
        for step in (5, 2, 3, 4):
            spread_rows(frame, step)
    wait_for(rt.at[1], r_recv.at[1])

    def dispatch(i):
        frame, g = i % 2, i // 2

        @pl.when(g == 0)
        def _():
            wait_for(tok.at[frame, 0, c, pl.ds(0, 3)], z_recv.at[frame, 0])

        @pl.when(g == 1)
        def _():
            wait_for(tok.at[frame, 1, c], z_recv.at[frame, 1])

        send(
            tok.at[frame, g, c], tok.at[frame, g, c],
            c_send.at[i], c_recv.at[i], pixel=z * 2 + 1 - c,
        )
        table = jnp.concatenate([rt[frame, g, 0], rt[frame, g, 1]], axis=1)
        hits, scales = [], []
        for j in range(SIDE):
            named = table[0:TOP] == (p * SIDE + j).astype(F32)
            hits.append(jnp.sum(named.astype(F32), axis=0, keepdims=True))
            scales.append(
                jnp.sum(jnp.where(named, table[8 : 8 + TOP], 0.0), axis=0, keepdims=True)
            )
        lanes = (GROUP, GROUP)
        before = (iota(lanes, 0) <= iota(lanes, 1)) & (
            iota(lanes, 0) // HERE == iota(lanes, 1) // HERE
        )
        hit = jnp.concatenate(hits + hits, axis=0)
        rank = dot(hit.astype(BF16), before.astype(BF16))
        base = (iota((1, GROUP), 1) // HERE * CAP).astype(F32) - 1.0
        number = iota((SLOTS, GROUP), 0).astype(F32)
        chosen, scaled = [], []
        for j in range(SIDE):
            slot = jnp.where(hits[j] > 0.5, base + rank[j : j + 1], -1.0)
            match = number == slot
            chosen.append(jnp.where(match, 1.0, 0.0))
            scaled.append(jnp.where(match, scales[j], 0.0))
        sel[...] = jnp.concatenate(chosen, axis=0).astype(BF16)
        spr[i] = jnp.transpose(jnp.concatenate(scaled, axis=0)).astype(BF16)
        wait_for(tok.at[frame, g, 1 - c], c_recv.at[i])

        def columns(n):
            at = pl.ds(pl.multiple_of(n * CHUNK, CHUNK), CHUNK)
            block = tok[frame, g, :, :, :, at].reshape(GROUP, CHUNK)
            rows_out[i, :, :, at] = (
                dot(sel[...], block).astype(BF16).reshape(SIDE, SLOTS, CHUNK)
            )

        loop(0, D // CHUNK, columns)
        for step in range(1, SIDE):
            to = (y + step) % SIDE
            send(
                rows_out.at[i, to], arrive.at[i, y], y_send.at[i], y_recv.at[i], frame=at_y(to)
            )
        arrive[i, y] = rows_out[i, y]

    def give_back(i):
        for step in range(1, SIDE):
            to = (y + step) % SIDE
            send(parts.at[i, to], back.at[i, y], b_send.at[i], b_recv.at[i], frame=at_y(to))

    def feed_forward(i):
        wait_for(arrive.at[i, pl.ds(0, SIDE - 1)], y_recv.at[i])
        flat = arrive[i].reshape(SIDE * SLOTS, D)

        def active(hidden, width, at):
            return (jax.nn.silu(hidden[:, :width]) * hidden[:, at : at + width]).astype(BF16)

        act_own = active(dot(flat, own_al[...]), FF_PAD, FF_PAD)
        act_left = active(dot(flat, left_gu[...]), HALF, HALF)
        act_right = active(dot(flat, right_gu[...]), HALF, HALF)

        def columns(n):
            at = pl.ds(pl.multiple_of(n * CHUNK, CHUNK), CHUNK)
            total = (
                dot(act_own, own_dn[:, at])
                + dot(act_left, left_dn[:, at])
                + dot(act_right, right_dn[:, at])
            )
            parts[i, :, :, at] = total.astype(BF16).reshape(SIDE, SLOTS, CHUNK)

        loop(0, D // CHUNK, columns)
        back[i, y] = parts[i, y]

        @pl.when(i >= 2)
        def _():
            give_back(i)

    def forward(k):
        @pl.when(k < 4)
        def _():
            dispatch(k)

        @pl.when(k == 2)
        def _():
            wait_for(left_gu, w_recv.at[1])
            wait_for(right_gu, w_recv.at[0])
            wait_for(left_dn, w_recv.at[3])
            wait_for(right_dn, w_recv.at[2])

        @pl.when(k >= 2)
        def _():
            feed_forward(k - 2)

    loop(0, 6, forward)
    give_back(1)
    give_back(0)

    def combine(k):
        i = jnp.where(k < 2, k + 2, 3 - k)
        frame, g = i % 2, i // 2
        wait_for(back.at[i, pl.ds(0, SIDE - 1)], b_recv.at[i])

        def columns(n):
            at = pl.ds(pl.multiple_of(n * CHUNK, CHUNK), CHUNK)
            block = back[i, :, :, at].reshape(SIDE * SLOTS, CHUNK)
            mixed[i, :, :, :, at] = (
                dot(spr[i], block).astype(BF16).reshape(2, 4, HERE, CHUNK)
            )

        loop(0, D // CHUNK, columns)
        send(mixed.at[i, 1 - c], sib.at[i], m_send.at[i], m_recv.at[i], pixel=z * 2 + 1 - c)
        wait_for(sib.at[i], m_recv.at[i])

        def blocks(q):
            zred[i, q] = (mixed[i, c, q].astype(F32) + sib[i, q].astype(F32)).astype(BF16)

        loop(0, 4, blocks)

        def out(step):
            to = (z + step) % DEPTH
            send(
                zred.at[i, to % 4], zin.at[frame, z], q_send.at[frame, step], q_recv.at[frame],
                pixel=to * 2 + c,
            )

        @pl.when(g == 0)
        def _():
            for step in (2, 7, 1):
                out(step)
            zin[frame, z] = zred[i, spot]

        @pl.when(g == 1)
        def _():
            for step in (4, 3, 5, 6):
                out(step)

    loop(0, 4, combine)

    def total(frame):
        wait_for(zin.at[frame, pl.ds(0, DEPTH - 1)], q_recv.at[frame])
        result = zin[frame, 0].astype(F32)
        for q in range(1, DEPTH):
            result = result + zin[frame, q].astype(F32)
        return result

    fin_out[...] = total(1).astype(BF16)
    send(fin_out, fin_in, pair_send.at[1], pair_recv.at[1], frame=at_x(2))
    own_total = total(0)
    wait_for(fin_in, pair_recv.at[1])
    mix_out[...] = (own_total + fin_in[...].astype(F32)).astype(BF16)

    wait_for(piece_a, w_send.at[0])
    wait_for(piece_b, w_send.at[1])
    wait_for(right_dn, w_send.at[2])
    wait_for(left_dn, w_send.at[3])
    wait_for(s_out.at[:, pl.ds(0, 15)], a_send.at[0])
    wait_for(t_out.at[:, pl.ds(0, 15)], a_send.at[1])
    wait_for(s_part.at[pl.ds(0, 15)], a_send.at[2])
    wait_for(t_part.at[pl.ds(0, 15)], a_send.at[3])
    wait_for(r_in.at[pl.ds(0, 15)], r_send.at[0])
    wait_for(rt.at[0], r_send.at[1])
    wait_for(mine, pair_send.at[0])
    wait_for(fin_out, pair_send.at[1])

    def sent(i):
        for frame in range(2):
            wait_for(tok.at[0, 0, 0, 0], z_send.at[frame, i])
            wait_for(zred.at[0, 0], q_send.at[frame, i])

    loop(1, DEPTH, sent)

    def sent_groups(i):
        wait_for(tok.at[0, 0, 0], c_send.at[i])
        wait_for(rows_out.at[i, pl.ds(0, SIDE - 1)], y_send.at[i])
        wait_for(parts.at[i, pl.ds(0, SIDE - 1)], b_send.at[i])
        wait_for(mixed.at[i, 0], m_send.at[i])

    loop(0, 4, sent_groups)


def per_device(
    tokens,
    spatial_inputs,
    temporal_inputs,
    gate_spatial,
    gate_temporal,
    norm_gain,
    route_experts,
    route_weights,
    expert_gate_up,
    expert_down,
):
    vmem = pl.BlockSpec(memory_space=pltpu.VMEM)
    hbm = pl.BlockSpec(memory_space=pl.ANY)
    dma = pltpu.SemaphoreType.DMA

    def buf(*shape, dtype=BF16):
        return pltpu.VMEM(shape, dtype)

    attended, mix = pl.pallas_call(
        kernel,
        out_shape=[jax.ShapeDtypeStruct((HERE, D), BF16)] * 2,
        in_specs=[vmem] * 8 + [hbm] * 2,
        out_specs=[vmem] * 2,
        scratch_shapes=[
            buf(D, 2 * FF), buf(D, 2 * FF_PAD), buf(D, FF), buf(D, FF), buf(D, FF), buf(D, FF),
            buf(FF_PAD, D), buf(HALF, D), buf(HALF, D),
            buf(3, HEADS, HERE, HDIM), buf(3, HEADS, HERE, HDIM),
            buf(3, HEADS, HERE, HDIM), buf(3, HEADS, HERE, HDIM),
            buf(HEADS, HERE, HDIM), buf(HEADS, HERE, HDIM), buf(HERE, D), buf(HERE, D),
            buf(16, 128, dtype=F32), buf(16, 16, 128, dtype=F32),
            buf(2, 2, 2, 16, 128, dtype=F32),
            buf(2, 2, 2, 4, HERE, D),
            buf(GROUP, GROUP), buf(4, GROUP, GROUP),
            buf(4, SIDE, SLOTS, D), buf(4, SIDE, SLOTS, D), buf(4, SIDE, SLOTS, D),
            buf(4, SIDE, SLOTS, D),
            buf(4, 2, 4, HERE, D), buf(4, 4, HERE, D), buf(4, 4, HERE, D),
            buf(2, DEPTH, HERE, D),
            buf(HERE, D), buf(HERE, D),
            dma((2,)), dma((4,)), dma((4,)), dma((4,)), dma((4,)), dma((2,)), dma((2,)),
            dma((2,)), dma((2,)), dma((2, DEPTH)), dma((2, 2)), dma((4,)), dma((4,)),
            dma((4,)), dma((4,)), dma((4,)), dma((4,)), dma((4,)), dma((4,)),
            dma((2, DEPTH)), dma((2,)),
        ],
        compiler_params=pltpu.CompilerParams(
            collective_id=0, has_side_effects=True, vmem_limit_bytes=60 * 1024 * 1024
        ),
    )(
        tokens[0],
        spatial_inputs[0],
        temporal_inputs[0],
        gate_spatial[None],
        gate_temporal[None],
        norm_gain[None],
        route_experts[0],
        route_weights[0],
        expert_gate_up[0],
        expert_down[0],
    )
    return (attended[None], mix[None])


def solution(mesh):
    in_specs = (
        P("frame", "pixel", None),
        P("frame", "pixel", None),
        P("frame", "pixel", None),
        P(),
        P(),
        P(),
        P("frame", "pixel", None),
        P("frame", "pixel", None),
        P(("frame", "pixel"), None, None),
        P(("frame", "pixel"), None, None),
    )
    out_specs = (P("frame", "pixel", None), P("frame", "pixel", None))
    return jax.shard_map(
        per_device, mesh=mesh, in_specs=in_specs, out_specs=out_specs, check_vma=False
    )
```

time: 337 us -> 211 us (0.63)
  Pallas kernels: 0 us -> 198 us
  waiting for transfers between devices: 197 us -> 0 us
  starting transfers between devices: 44 us -> 0 us
  matrix products: 34.7 us -> 0 us
  blocking collectives: 18.4 us -> 0 us
  between operations: 14.4 us -> 0.64 us
  other arithmetic: 10.8 us -> 0 us
    pallas_call x0 -> x1, Pallas kernels: none -> 198 us  [per_device(): pl.pallas_call(kernel, out_shape=[jax.ShapeDtypeStruct((HERE, D), BF16)]...]
    all_to_all x6 -> x0, waiting for transfers between devices: 121 us -> none  [the longest x1 47.3 us: per_device(): lax.all_to_all(parts, 'frame', split_axis=0, concat_axis=0, tiled=True, a...]
    reduce_scatter x1 -> x0, waiting for transfers between devices: 57.5 us -> none  [per_device(): mixed = lax.psum_scatter(mixed, 'pixel', scatter_dimension=1, tiled=True)]
    all_to_all x6 -> x0, starting transfers between devices: 35 us -> none  [the longest x1 10.3 us: per_device(): lax.all_to_all(spatial_packed, 'pixel', split_axis=2, concat_axis=0, tile...]
    dot_general x11 -> x0, matrix products: 31.3 us -> none  [the longest x3 13.7 us: partial(): both_halves = jnp.dot(flat, gate_up, preferred_element_type=jnp.float32)]
    all_gather x1 -> x0, blocking collectives: 18.4 us -> none  [per_device(): routing = lax.all_gather(routing, 'pixel', axis=1, tiled=True)]
    ppermute x7 -> x0, waiting for transfers between devices: 11.3 us -> none  [the longest x1 5.36 us: per_device(): lax.ppermute(expert_input, 'frame', shift(2))]
    ppermute x7 -> x0, starting transfers between devices: 8.98 us -> none  [the longest x1 2.77 us: per_device(): other = lax.ppermute(mixed[1], 'frame', shift(2))]
  transfers between devices with their start and end apart: 15 -> 0, of which waited for: 11 -> 0; matrix products, arithmetic and copies ran while one was open for 11% -> 0% of each run, Pallas kernels for 0% -> 0%
where the time goes in v2:
time: 211 us; the launch traced here: 209 us
  Pallas kernels  198 us (94%)
  local copies, waits for them, and re-layouts  10.5 us (5%)
    pallas_call x1, Pallas kernels, per_device(): pl.pallas_call(kernel, out_shape=[jax.ShapeDtypeStruct((HERE, D), BF16)]...  198 us
    unnamed x5, local copies, waits for them, and re-layouts  10.5 us

profile of v2, /device:TPU:1, one launch (start us, length us, event | category | flops | bytes accessed | tf_op | source)
XLA Modules:
  0.0 209.1 jit_solution(3820432919261268215)
XLA Ops:
  0.6 1.4 copy.12
  2.0 1.4 copy.13
  3.4 4.6 %copy.14 = bf16[1,2048,704]{2,1,0:T(8,128)(2,1)} copy(bf16[1,2048,704]{1,2,0:T(8,128)(2,1)} %param.18) | data formatting | bytes 5767168 | tf_op args[8]
  8.0 198.0 %shard_map.113 = (bf16[32,2048]{1,0:T(8,128)(2,1)}, bf16[32,2048]{1,0:T(8,128)(2,1)}) custom-call(bf16[32,2048]{1,0:T(8,128)(2,1)} %bitcast.16, bf16[32,6144]{1,0:T(8,128)(2,1)} %bitcast.14, bf16[32,6144]{1,0:T(8,128)(2,1)} %bitcast.15, f32[1,2048]{1,0:T(1,128)} %bitcast.21, f32[1,2048]{1,0:T(1,128)} %bitcast.22, f32[1,2048]{1,0:T(1,128)} %bitcast.23, ...), custom_call_target="tpu_custom_call" | custom-call | tf_op jit(solution)/shard_map/pallas_call | solution.py:454
  206.0 1.6 copy.17
  207.5 1.6 copy.18

commit v3 on v2

--- a/solution.py
+++ b/solution.py
@@ -18,7 +18,7 @@
 HERE = 32
 FF = 352
 HALF = FF // 2
-FF_PAD = 384
+FF_PAD = 768
 GROUP = 8 * HERE
 SLOTS = GROUP // HERE * CAP
 CHUNK = 512
@@ -77,7 +77,7 @@
 def kernel(
     tokens, spatial, temporal, gate_s, gate_t, gain, experts, weights, gate_up, down,
     attended_out, mix_out,
-    own_gu, own_al, piece_a, piece_b, left_gu, right_gu, own_dn, left_dn, right_dn,
+    gu_all, dn_all, act,
     s_out, s_in, t_out, t_in, s_part, t_part, s_ret, t_ret,
     r_out, r_in, rt, tok, sel, spr, rows_out, arrive, parts, back, mixed, sib, zred, zin,
     fin_out, fin_in,
@@ -97,10 +97,15 @@
     def at_y(other):
         return other * SIDE + x
 
-    load_gu = pltpu.make_async_copy(gate_up, own_gu, load_sem.at[0])
-    load_dn = pltpu.make_async_copy(down, own_dn.at[pl.ds(0, FF)], load_sem.at[1])
-    load_gu.start()
-    load_dn.start()
+    loads = [
+        pltpu.make_async_copy(gate_up.at[pl.ds(0, FF)], gu_all.at[pl.ds(0, FF)], load_sem.at[0]),
+        pltpu.make_async_copy(
+            gate_up.at[pl.ds(FF, FF)], gu_all.at[pl.ds(FF_PAD, FF)], load_sem.at[1]
+        ),
+        pltpu.make_async_copy(down, dn_all.at[pl.ds(0, FF)], load_sem.at[2]),
+    ]
+    for load in loads:
+        load.start()
 
     barrier = pltpu.get_barrier_semaphore()
 
@@ -121,10 +126,10 @@
             t_out[w, h] = temporal[:, at : at + HDIM]
     place = (iota((HERE, 128), 1) == iota((HERE, 128), 0) + spot * HERE).astype(F32)
     exact = dict(precision=lax.Precision.HIGHEST, preferred_element_type=F32)
-    over = (((0,), (0,)), ((), ()))
+    over = (((1,), (0,)), ((), ()))
     r_out[...] = jnp.zeros_like(r_out)
-    r_out[0:TOP] = lax.dot_general(experts[...].astype(F32), place, over, **exact)
-    r_out[8 : 8 + TOP] = lax.dot_general(weights[...], place, over, **exact)
+    r_out[0:TOP] = lax.dot_general(experts[:, 0].astype(F32), place, over, **exact)
+    r_out[8 : 8 + TOP] = lax.dot_general(weights[:, 0], place, over, **exact)
 
     pl.semaphore_wait(barrier, 30)
 
@@ -143,30 +148,17 @@
     t_in[:, f] = t_out[:, f]
     r_in[p] = r_out[...]
 
-    load_gu.wait()
-    load_dn.wait()
-    own_dn[FF:FF_PAD] = jnp.zeros((FF_PAD - FF, D), BF16)
-    src, dst = iota((2 * FF, FF), 0), iota((2 * FF, FF), 1)
-    pick_a = (src == jnp.where(dst < HALF, dst, dst + HALF)).astype(BF16)
-    pick_b = (src == jnp.where(dst < HALF, dst + HALF, dst + 2 * HALF)).astype(BF16)
-    src, dst = iota((2 * FF, 2 * FF_PAD), 0), iota((2 * FF, 2 * FF_PAD), 1)
-    pick_al = (
-        ((dst < FF) & (src == dst)) | ((dst >= FF_PAD) & (src == dst - FF_PAD + FF))
-    ).astype(BF16)
-
-    def cut(i):
-        rows = pl.ds(i * 256, 256)
-        block = own_gu[rows]
-        piece_a[rows] = dot(block, pick_a).astype(BF16)
-        piece_b[rows] = dot(block, pick_b).astype(BF16)
-
-    loop(0, 8, cut)
-    send(piece_a, right_gu, w_send.at[0], w_recv.at[0], frame=at_x(3))
-    send(piece_b, left_gu, w_send.at[1], w_recv.at[1], frame=at_x(1))
-    send(own_dn.at[pl.ds(0, HALF)], right_dn, w_send.at[2], w_recv.at[2], frame=at_x(3))
-    send(own_dn.at[pl.ds(HALF, HALF)], left_dn, w_send.at[3], w_recv.at[3], frame=at_x(1))
-
     wait_for(t_in.at[:, pl.ds(0, 15)], a_recv.at[1])
+
+    for side, to, first, last in ((0, at_x(3), 0, FF + HALF), (1, at_x(1), HALF, FF)):
+        for part, (source, start, target, base) in enumerate((
+            (gate_up, first, gu_all, 0), (gate_up, FF + first, gu_all, FF_PAD),
+            (down, first, dn_all, 0),
+        )):
+            send(
+                source.at[pl.ds(start, HALF)], target.at[pl.ds(base + last, HALF)],
+                w_send.at[side, part], w_recv.at[side, part], frame=to,
+            )
     attend(t_in, t_part, True)
 
     def return_t(i):
@@ -202,11 +194,12 @@
             rt[0, g, core] = total
     send(rt.at[0], rt.at[1], r_send.at[1], r_recv.at[1], frame=at_x(2))
 
-    def align(i):
-        rows = pl.ds(i * 256, 256)
-        own_al[rows] = dot(own_gu[rows], pick_al).astype(BF16)
-
-    loop(0, 8, align)
+    for load in loads:
+        load.wait()
+    pad = 2 * FF
+    gu_all[pad:FF_PAD] = jnp.zeros((FF_PAD - pad, D), BF16)
+    gu_all[FF_PAD + pad :] = jnp.zeros((FF_PAD - pad, D), BF16)
+    dn_all[pad:] = jnp.zeros((FF_PAD - pad, D), BF16)
 
     wait_for(t_ret.at[:, pl.ds(0, 15 * HDIM)], a_recv.at[3])
     wait_for(s_ret.at[:, pl.ds(0, 15 * HDIM)], a_recv.at[2])
@@ -306,20 +299,18 @@
         wait_for(arrive.at[i, pl.ds(0, SIDE - 1)], y_recv.at[i])
         flat = arrive[i].reshape(SIDE * SLOTS, D)
 
-        def active(hidden, width, at):
-            return (jax.nn.silu(hidden[:, :width]) * hidden[:, at : at + width]).astype(BF16)
-
-        act_own = active(dot(flat, own_al[...]), FF_PAD, FF_PAD)
-        act_left = active(dot(flat, left_gu[...]), HALF, HALF)
-        act_right = active(dot(flat, right_gu[...]), HALF, HALF)
+        def hidden(n):
+            gate = dot(flat, gu_all[pl.ds(n * GROUP, GROUP)], (1, 1))
+            up = dot(flat, gu_all[pl.ds(FF_PAD + n * GROUP, GROUP)], (1, 1))
+            act[n] = (jax.nn.silu(gate) * up).astype(BF16)
+
+        loop(0, FF_PAD // GROUP, hidden)
 
         def columns(n):
             at = pl.ds(pl.multiple_of(n * CHUNK, CHUNK), CHUNK)
-            total = (
-                dot(act_own, own_dn[:, at])
-                + dot(act_left, left_dn[:, at])
-                + dot(act_right, right_dn[:, at])
-            )
+            total = dot(act[0], dn_all[0:GROUP, at])
+            for m in range(1, FF_PAD // GROUP):
+                total = total + dot(act[m], dn_all[m * GROUP : (m + 1) * GROUP, at])
             parts[i, :, :, at] = total.astype(BF16).reshape(SIDE, SLOTS, CHUNK)
 
         loop(0, D // CHUNK, columns)
@@ -336,10 +327,9 @@
 
         @pl.when(k == 2)
         def _():
-            wait_for(left_gu, w_recv.at[1])
-            wait_for(right_gu, w_recv.at[0])
-            wait_for(left_dn, w_recv.at[3])
-            wait_for(right_dn, w_recv.at[2])
+            for side in range(2):
+                for part in range(3):
+                    wait_for(dn_all.at[pl.ds(0, HALF)], w_recv.at[side, part])
 
         @pl.when(k >= 2)
         def _():
@@ -403,10 +393,9 @@
     wait_for(fin_in, pair_recv.at[1])
     mix_out[...] = (own_total + fin_in[...].astype(F32)).astype(BF16)
 
-    wait_for(piece_a, w_send.at[0])
-    wait_for(piece_b, w_send.at[1])
-    wait_for(right_dn, w_send.at[2])
-    wait_for(left_dn, w_send.at[3])
+    for side in range(2):
+        for part in range(3):
+            wait_for(dn_all.at[pl.ds(0, HALF)], w_send.at[side, part])
     wait_for(s_out.at[:, pl.ds(0, 15)], a_send.at[0])
     wait_for(t_out.at[:, pl.ds(0, 15)], a_send.at[1])
     wait_for(s_part.at[pl.ds(0, 15)], a_send.at[2])
@@ -457,8 +446,7 @@
         in_specs=[vmem] * 8 + [hbm] * 2,
         out_specs=[vmem] * 2,
         scratch_shapes=[
-            buf(D, 2 * FF), buf(D, 2 * FF_PAD), buf(D, FF), buf(D, FF), buf(D, FF), buf(D, FF),
-            buf(FF_PAD, D), buf(HALF, D), buf(HALF, D),
+            buf(2 * FF_PAD, D), buf(FF_PAD, D), buf(FF_PAD // GROUP, GROUP, GROUP),
             buf(3, HEADS, HERE, HDIM), buf(3, HEADS, HERE, HDIM),
             buf(3, HEADS, HERE, HDIM), buf(3, HEADS, HERE, HDIM),
             buf(HEADS, HERE, HDIM), buf(HEADS, HERE, HDIM), buf(HERE, D), buf(HERE, D),
@@ -471,7 +459,7 @@
             buf(4, 2, 4, HERE, D), buf(4, 4, HERE, D), buf(4, 4, HERE, D),
             buf(2, DEPTH, HERE, D),
             buf(HERE, D), buf(HERE, D),
-            dma((2,)), dma((4,)), dma((4,)), dma((4,)), dma((4,)), dma((2,)), dma((2,)),
+            dma((3,)), dma((2, 3)), dma((2, 3)), dma((4,)), dma((4,)), dma((2,)), dma((2,)),
             dma((2,)), dma((2,)), dma((2, DEPTH)), dma((2, 2)), dma((4,)), dma((4,)),
             dma((4,)), dma((4,)), dma((4,)), dma((4,)), dma((4,)), dma((4,)),
             dma((2, DEPTH)), dma((2,)),
@@ -486,9 +474,9 @@
         gate_spatial[None],
         gate_temporal[None],
         norm_gain[None],
-        route_experts[0],
-        route_weights[0],
-        expert_gate_up[0],
+        jnp.transpose(route_experts, (2, 0, 1)),
+        jnp.transpose(route_weights, (2, 0, 1)),
+        jnp.transpose(expert_gate_up, (0, 2, 1))[0],
         expert_down[0],
     )
     return (attended[None], mix[None])

time: 211 us -> 203 us (0.962)
  local copies, waits for them, and re-layouts: 10.5 us -> 3.14 us
    unnamed x5 -> x2, local copies, waits for them, and re-layouts: 10.5 us -> 3.14 us
where the time goes in v3:
time: 203 us
  Pallas kernels  199 us (98%)
  local copies, waits for them, and re-layouts  3.14 us (2%)
    pallas_call x1, Pallas kernels, per_device(): pl.pallas_call(kernel, out_shape=[jax.ShapeDtypeStruct((HERE, D), BF16)]...  199 us

profile of v3, /device:TPU:1, one launch (start us, length us, event | category | flops | bytes accessed | tf_op | source)
XLA Modules:
  0.0 202.5 jit_solution(10132339096652300928)
XLA Ops:
  0.6 198.7 %shard_map.113 = (bf16[32,2048]{1,0:T(8,128)(2,1)}, bf16[32,2048]{1,0:T(8,128)(2,1)}) custom-call(bf16[32,2048]{1,0:T(8,128)(2,1)} %bitcast.18, bf16[32,6144]{1,0:T(8,128)(2,1)} %bitcast.16, bf16[32,6144]{1,0:T(8,128)(2,1)} %bitcast.17, f32[1,2048]{1,0:T(1,128)} %bitcast.21, f32[1,2048]{1,0:T(1,128)} %bitcast.22, f32[1,2048]{1,0:T(1,128)} %bitcast.23, ...), custom_call_target="tpu_custom_call" | custom-call | tf_op jit(solution)/shard_map/pallas_call | solution.py:443
  199.4 1.6 copy.14
  200.9 1.6 copy.15

commit v4 on v3

--- a/solution.py
+++ b/solution.py
@@ -80,7 +80,7 @@
     gu_all, dn_all, act,
     s_out, s_in, t_out, t_in, s_part, t_part, s_ret, t_ret,
     r_out, r_in, rt, tok, sel, spr, rows_out, arrive, parts, back, mixed, sib, zred, zin,
-    fin_out, fin_in,
+    zfar, fin_out, fin_in,
     load_sem, w_send, w_recv, a_send, a_recv, r_send, r_recv, pair_send, pair_recv,
     z_send, z_recv, c_send, c_recv, y_send, y_recv, b_send, b_recv, m_send, m_recv,
     q_send, q_recv,
@@ -150,15 +150,6 @@
 
     wait_for(t_in.at[:, pl.ds(0, 15)], a_recv.at[1])
 
-    for side, to, first, last in ((0, at_x(3), 0, FF + HALF), (1, at_x(1), HALF, FF)):
-        for part, (source, start, target, base) in enumerate((
-            (gate_up, first, gu_all, 0), (gate_up, FF + first, gu_all, FF_PAD),
-            (down, first, dn_all, 0),
-        )):
-            send(
-                source.at[pl.ds(start, HALF)], target.at[pl.ds(base + last, HALF)],
-                w_send.at[side, part], w_recv.at[side, part], frame=to,
-            )
     attend(t_in, t_part, True)
 
     def return_t(i):
@@ -170,6 +161,18 @@
 
     loop(1, 16, return_t)
     t_ret[:, pl.ds(pl.multiple_of(f * HDIM, HDIM), HDIM)] = t_part[f]
+
+    def share(part):
+        source, start, target, base = (
+            (gate_up, 0, gu_all, 0), (gate_up, FF, gu_all, FF_PAD), (down, 0, dn_all, 0)
+        )[part]
+        for side, to, first, last in ((0, at_x(3), 0, FF + HALF), (1, at_x(1), HALF, FF)):
+            send(
+                source.at[pl.ds(start + first, HALF)], target.at[pl.ds(base + last, HALF)],
+                w_send.at[side, part], w_recv.at[side, part], frame=to,
+            )
+
+    share(0)
 
     wait_for(s_in.at[:, pl.ds(0, 15)], a_recv.at[0])
     attend(s_in, s_part, False)
@@ -216,22 +219,29 @@
     mine, other = tok.at[0, 0, c, spot], tok.at[1, 0, c, spot]
     send(mine, other, pair_send.at[0], pair_recv.at[0], frame=at_x(2))
 
-    def spread_rows(frame, step):
-        to = (z + step) % DEPTH
-        group = (((DEPTH - step) + 1) % DEPTH) // 4
-        send(
-            tok.at[frame, 0, c, spot], tok.at[frame, group, c, spot],
-            z_send.at[frame, step], z_recv.at[frame, group], pixel=to * 2 + c,
-        )
-
-    for step in (1, 7, 6):
-        spread_rows(0, step)
+    def spread_near(frame):
+        for step, way in ((7, 1), (1, 0), (6, 2)):
+            at = spot
+            send(
+                tok.at[frame, 0, c, at], tok.at[frame, 0, c, at],
+                z_send.at[frame, way], z_recv.at[frame, 0],
+                pixel=(z + step) % DEPTH * 2 + c,
+            )
+
+    def spread_far(frame):
+        for way, (block, step) in enumerate(((2, 7), (7, 1), (2, 6), (7, 2))):
+            at = (z + block) % 4
+            send(
+                tok.at[frame, 0, c, at], tok.at[frame, 1, c, at],
+                z_send.at[frame, 3 + way], z_recv.at[frame, 1],
+                pixel=(z + step) % DEPTH * 2 + c,
+            )
+
+    spread_near(0)
     wait_for(other, pair_recv.at[0])
-    for step in (1, 7, 6):
-        spread_rows(1, step)
-    for frame in range(2):
-        for step in (5, 2, 3, 4):
-            spread_rows(frame, step)
+    spread_near(1)
+    share(1)
+    share(2)
     wait_for(rt.at[1], r_recv.at[1])
 
     def dispatch(i):
@@ -240,6 +250,7 @@
         @pl.when(g == 0)
         def _():
             wait_for(tok.at[frame, 0, c, pl.ds(0, 3)], z_recv.at[frame, 0])
+            spread_far(frame)
 
         @pl.when(g == 1)
         def _():
@@ -315,32 +326,19 @@
 
         loop(0, D // CHUNK, columns)
         back[i, y] = parts[i, y]
-
-        @pl.when(i >= 2)
-        def _():
-            give_back(i)
-
-    def forward(k):
-        @pl.when(k < 4)
-        def _():
-            dispatch(k)
-
-        @pl.when(k == 2)
-        def _():
-            for side in range(2):
-                for part in range(3):
-                    wait_for(dn_all.at[pl.ds(0, HALF)], w_recv.at[side, part])
-
-        @pl.when(k >= 2)
-        def _():
-            feed_forward(k - 2)
-
-    loop(0, 6, forward)
-    give_back(1)
-    give_back(0)
+        give_back(i)
+
+    def order(k):
+        return jnp.where(k < 2, k + 2, 3 - k)
+
+    loop(0, 4, dispatch)
+    for side in range(2):
+        for part in range(3):
+            wait_for(dn_all.at[pl.ds(0, HALF)], w_recv.at[side, part])
+    loop(0, 4, lambda k: feed_forward(order(k)))
 
     def combine(k):
-        i = jnp.where(k < 2, k + 2, 3 - k)
+        i = order(k)
         frame, g = i % 2, i // 2
         wait_for(back.at[i, pl.ds(0, SIDE - 1)], b_recv.at[i])
 
@@ -355,35 +353,46 @@
         send(mixed.at[i, 1 - c], sib.at[i], m_send.at[i], m_recv.at[i], pixel=z * 2 + 1 - c)
         wait_for(sib.at[i], m_recv.at[i])
 
-        def blocks(q):
-            zred[i, q] = (mixed[i, c, q].astype(F32) + sib[i, q].astype(F32)).astype(BF16)
-
-        loop(0, 4, blocks)
-
-        def out(step):
-            to = (z + step) % DEPTH
+        def put(q, value):
+            zred[i, q] = value.astype(BF16)
+
+        def summed(q):
+            return mixed[i, c, q].astype(F32) + sib[i, q].astype(F32)
+
+        def out(way, block, step, target):
             send(
-                zred.at[i, to % 4], zin.at[frame, z], q_send.at[frame, step], q_recv.at[frame],
-                pixel=to * 2 + c,
-            )
+                zred.at[i, (z + block) % 4], target, q_send.at[frame, way],
+                q_recv.at[frame, g], pixel=(z + step) % DEPTH * 2 + c,
+            )
+
+        @pl.when(g == 1)
+        def _():
+            loop(0, 4, lambda q: put(q, summed(q)))
+            out(3, 6, 7, zfar.at[frame, 0, 0])
+            out(4, 3, 1, zfar.at[frame, 1, 0])
+            out(5, 5, 6, zfar.at[frame, 0, 1])
+            out(6, 4, 2, zfar.at[frame, 1, 1])
 
         @pl.when(g == 0)
         def _():
-            for step in (2, 7, 1):
-                out(step)
-            zin[frame, z] = zred[i, spot]
-
-        @pl.when(g == 1)
-        def _():
-            for step in (4, 3, 5, 6):
-                out(step)
+            wait_for(zfar.at[frame], q_recv.at[frame, 1])
+            for side, block in ((1, 2), (0, 7)):
+                q = (z + block) % 4
+                far = zfar[frame, side, 0].astype(F32) + zfar[frame, side, 1].astype(F32)
+                put(q, summed(q) + far)
+            out(0, 2, 2, zin.at[frame, 0])
+            out(1, 7, 7, zin.at[frame, 1])
+            q = (z + 1) % 4
+            put(q, summed(q))
+            out(2, 1, 1, zin.at[frame, 2])
+            zred[i, spot] = summed(spot).astype(BF16)
 
     loop(0, 4, combine)
 
     def total(frame):
-        wait_for(zin.at[frame, pl.ds(0, DEPTH - 1)], q_recv.at[frame])
-        result = zin[frame, 0].astype(F32)
-        for q in range(1, DEPTH):
+        wait_for(zin.at[frame], q_recv.at[frame, 0])
+        result = zred[frame, spot].astype(F32)
+        for q in range(3):
             result = result + zin[frame, q].astype(F32)
         return result
 
@@ -410,7 +419,7 @@
             wait_for(tok.at[0, 0, 0, 0], z_send.at[frame, i])
             wait_for(zred.at[0, 0], q_send.at[frame, i])
 
-    loop(1, DEPTH, sent)
+    loop(0, 7, sent)
 
     def sent_groups(i):
         wait_for(tok.at[0, 0, 0], c_send.at[i])
@@ -457,12 +466,12 @@
             buf(4, SIDE, SLOTS, D), buf(4, SIDE, SLOTS, D), buf(4, SIDE, SLOTS, D),
             buf(4, SIDE, SLOTS, D),
             buf(4, 2, 4, HERE, D), buf(4, 4, HERE, D), buf(4, 4, HERE, D),
-            buf(2, DEPTH, HERE, D),
+            buf(2, 3, HERE, D), buf(2, 2, 2, HERE, D),
             buf(HERE, D), buf(HERE, D),
             dma((3,)), dma((2, 3)), dma((2, 3)), dma((4,)), dma((4,)), dma((2,)), dma((2,)),
-            dma((2,)), dma((2,)), dma((2, DEPTH)), dma((2, 2)), dma((4,)), dma((4,)),
+            dma((2,)), dma((2,)), dma((2, 7)), dma((2, 2)), dma((4,)), dma((4,)),
             dma((4,)), dma((4,)), dma((4,)), dma((4,)), dma((4,)), dma((4,)),
-            dma((2, DEPTH)), dma((2,)),
+            dma((2, 7)), dma((2, 2)),
         ],
         compiler_params=pltpu.CompilerParams(
             collective_id=0, has_side_effects=True, vmem_limit_bytes=60 * 1024 * 1024

time: 203 us -> 157 us (0.77)
  Pallas kernels: 199 us -> 153 us
    pallas_call x1, Pallas kernels: 199 us -> 153 us  [per_device(): pl.pallas_call(kernel, out_shape=[jax.ShapeDtypeStruct((HERE, D), BF16)]...]
where the time goes in v4:
time: 157 us
  Pallas kernels  153 us (97%)
  local copies, waits for them, and re-layouts  3.14 us (2%)
    pallas_call x1, Pallas kernels, per_device(): pl.pallas_call(kernel, out_shape=[jax.ShapeDtypeStruct((HERE, D), BF16)]...  153 us

profile of v4, /device:TPU:1, one launch (start us, length us, event | category | flops | bytes accessed | tf_op | source)
XLA Modules:
  0.0 157.0 jit_solution(15773837765230630356)
XLA Ops:
  0.6 153.2 %shard_map.113 = (bf16[32,2048]{1,0:T(8,128)(2,1)}, bf16[32,2048]{1,0:T(8,128)(2,1)}) custom-call(bf16[32,2048]{1,0:T(8,128)(2,1)} %bitcast.18, bf16[32,6144]{1,0:T(8,128)(2,1)} %bitcast.16, bf16[32,6144]{1,0:T(8,128)(2,1)} %bitcast.17, f32[1,2048]{1,0:T(1,128)} %bitcast.21, f32[1,2048]{1,0:T(1,128)} %bitcast.22, f32[1,2048]{1,0:T(1,128)} %bitcast.23, ...), custom_call_target="tpu_custom_call" | custom-call | tf_op jit(solution)/shard_map/pallas_call | solution.py:452
  153.9 1.6 copy.14
  155.4 1.6 copy.15

commit v5 on v3

v5 whole, which is shorter than its diff:
```python
import math

import jax
import jax.numpy as jnp
from jax import lax
from jax.experimental import pallas as pl
from jax.experimental.pallas import tpu as pltpu
from jax.sharding import PartitionSpec as P

BF16, F32 = jnp.bfloat16, jnp.float32
D = 2048
HEADS = 16
HDIM = 128
TOP = 6
CAP = 8
SIDE = 4
DEPTH = 8
HERE = 32
FF = 352
HALF = FF // 2
FF_PAD = 768
GROUP = 8 * HERE
SLOTS = GROUP // HERE * CAP
CHUNK = 512


def dot(a, b, dims=(1, 0)):
    return lax.dot_general(
        a, b, (((dims[0],), (dims[1],)), ((), ())), preferred_element_type=F32
    )


def iota(shape, axis):
    return lax.broadcasted_iota(jnp.int32, shape, axis)


def send(src, dst, send_sem, recv_sem, **where):
    pltpu.make_async_remote_copy(
        src_ref=src,
        dst_ref=dst,
        send_sem=send_sem,
        recv_sem=recv_sem,
        device_id=where,
        device_id_type=pl.DeviceIdType.MESH,
    ).start()


def wait_for(ref, sem):
    pltpu.make_async_copy(ref, ref, sem).wait()


def loop(low, high, body):
    def step(i, carry):
        body(i)
        return carry

    lax.fori_loop(low, high, step, 0)


def attend(packed, out, masked):
    def rows(i):
        queries = packed[0, pl.ds(4 * i, 4)].reshape(4 * HERE, HDIM)
        key_rows = packed[1].reshape(HEADS * HERE, HDIM)
        values = packed[2].reshape(HEADS * HERE, HDIM)
        scores = dot(queries, key_rows, (1, 1)) * (1.0 / math.sqrt(HDIM))
        if masked:
            same = iota(scores.shape, 0) % HERE == iota(scores.shape, 1) % HERE
            scores = jnp.where(same, scores, -1e30)
        weights = jnp.exp(scores - jnp.max(scores, axis=-1, keepdims=True))
        total = jnp.sum(weights, axis=-1, keepdims=True)
        result = dot(weights.astype(BF16), values) / total
        out[pl.ds(4 * i, 4)] = result.astype(BF16).reshape(4, HERE, HDIM)

    loop(0, 4, rows)


def kernel(
    tokens_in, spatial_in, temporal_in, gate_s, gate_t, gain, experts, weights, gate_up, down,
    attended_out, mix_out,
    tokens, spatial, temporal, gu_all, dn_all, act,
    s_out, s_in, t_out, t_in, s_part, t_part, s_ret, t_ret,
    r_out, r_in, rt, tok, sel, spr, rows_out, arrive, parts, back, mixed, sib, zred, zin,
    zfar, fin_out, fin_in, xin,
    load_sem, w_send, w_recv, a_send, a_recv, r_send, r_recv, pair_send, pair_recv,
    z_send, z_recv, c_send, c_recv, y_send, y_recv, b_send, b_recv, m_send, m_recv,
    q_send, q_recv, l_send, l_recv, nb_send, nb_recv, nm_send, nm_recv, nq_send, nq_recv,
):
    f = lax.axis_index("frame")
    p = lax.axis_index("pixel")
    y, x = f // SIDE, f % SIDE
    z, c = p // 2, p % 2
    spot = z % 4

    def at_x(step):
        return y * SIDE + (x + step) % SIDE

    def at_y(other):
        return other * SIDE + x

    barrier = pltpu.get_barrier_semaphore()

    def greet(i):
        pl.semaphore_signal(
            barrier, inc=1, device_id={"pixel": (p + i) % 16}, device_id_type=pl.DeviceIdType.MESH
        )
        pl.semaphore_signal(
            barrier, inc=1, device_id={"frame": (f + i) % 16}, device_id_type=pl.DeviceIdType.MESH
        )

    loop(1, 16, greet)

    loads = [
        pltpu.make_async_copy(source, target, load_sem.at[n])
        for n, (source, target) in enumerate((
            (spatial_in, spatial), (temporal_in, temporal), (tokens_in, tokens),
            (gate_up.at[pl.ds(0, FF)], gu_all.at[pl.ds(0, FF)]),
            (gate_up.at[pl.ds(FF, FF)], gu_all.at[pl.ds(FF_PAD, FF)]),
            (down, dn_all.at[pl.ds(0, FF)]),
        ))
    ]
    for load in loads:
        load.start()
    for load in loads[:2]:
        load.wait()
    for w in range(3):
        for h in range(HEADS):
            at = (w * HEADS + h) * HDIM
            s_out[w, h] = spatial[:, at : at + HDIM]
            t_out[w, h] = temporal[:, at : at + HDIM]
    place = (iota((HERE, 128), 1) == iota((HERE, 128), 0) + spot * HERE).astype(F32)
    exact = dict(precision=lax.Precision.HIGHEST, preferred_element_type=F32)
    over = (((1,), (0,)), ((), ()))
    blank = jnp.zeros((8 - TOP, 128), F32)
    r_out[...] = jnp.concatenate([
        lax.dot_general(experts[:, 0].astype(F32), place, over, **exact), blank,
        lax.dot_general(weights[:, 0], place, over, **exact), blank,
    ], axis=0).astype(BF16)

    pl.semaphore_wait(barrier, 30)

    def scatter_heads(i):
        to_f, to_p = (f + i) % 16, (p + i) % 16
        send(t_out.at[:, to_f], t_in.at[:, f], a_send.at[1], a_recv.at[1], frame=to_f)
        send(s_out.at[:, to_p], s_in.at[:, p], a_send.at[0], a_recv.at[0], pixel=to_p)

    loop(1, 16, scatter_heads)

    s_in[:, p] = s_out[:, p]
    t_in[:, f] = t_out[:, f]
    r_in[p] = r_out[...]

    shares = (
        (gate_up, 0, gu_all, 0, 0, 96), (gate_up, 0, gu_all, 0, 96, HALF - 96),
        (gate_up, FF, gu_all, FF_PAD, 0, HALF), (down, 0, dn_all, 0, 0, HALF),
    )

    def share(part):
        source, start, target, base, skip, count = shares[part]
        for side, to, first, last in ((0, at_x(3), 0, FF + HALF), (1, at_x(1), HALF, FF)):
            send(
                source.at[pl.ds(start + first + skip, count)],
                target.at[pl.ds(base + last + skip, count)],
                w_send.at[side, part], w_recv.at[side, part], frame=to,
            )

    share(0)

    wait_for(t_in.at[:, pl.ds(0, 15)], a_recv.at[1])

    attend(t_in, t_part, True)

    def return_t(i):
        to = (f + i) % 16
        send(
            t_part.at[to], t_ret.at[:, pl.ds(pl.multiple_of(f * HDIM, HDIM), HDIM)],
            a_send.at[3], a_recv.at[3], frame=to,
        )

    loop(1, 16, return_t)
    t_ret[:, pl.ds(pl.multiple_of(f * HDIM, HDIM), HDIM)] = t_part[f]

    share(1)
    wait_for(s_in.at[:, pl.ds(0, 15)], a_recv.at[0])

    def scatter_routes(i):
        send(r_out, r_in.at[p], r_send.at[0], r_recv.at[0], pixel=(p + i) % 16)

    loop(1, 16, scatter_routes)
    attend(s_in, s_part, False)

    def return_s(i):
        to = (p + i) % 16
        send(
            s_part.at[to], s_ret.at[:, pl.ds(pl.multiple_of(p * HDIM, HDIM), HDIM)],
            a_send.at[2], a_recv.at[2], pixel=to,
        )

    loop(1, 16, return_s)
    s_ret[:, pl.ds(pl.multiple_of(p * HDIM, HDIM), HDIM)] = s_part[p]

    wait_for(r_in.at[pl.ds(0, 15)], r_recv.at[0])
    for g in range(2):
        for core in range(2):
            total = None
            for q in range(4):
                block = r_in[(z + 7 + 4 * g + q) % DEPTH * 2 + core].astype(F32)
                total = block if total is None else total + block
            rt[0, g, core] = total.astype(BF16)
    send(rt.at[0], rt.at[1], r_send.at[1], r_recv.at[1], frame=at_x(2))

    for load in loads[2:]:
        load.wait()
    pad = 2 * FF
    gu_all[pad:FF_PAD] = jnp.zeros((FF_PAD - pad, D), BF16)
    gu_all[FF_PAD + pad :] = jnp.zeros((FF_PAD - pad, D), BF16)
    dn_all[pad:] = jnp.zeros((FF_PAD - pad, D), BF16)

    def build(i):
        frame, g = i % 2, i // 2
        table = jnp.concatenate([rt[frame, g, 0], rt[frame, g, 1]], axis=1).astype(F32)
        hits, scales = [], []
        for j in range(SIDE):
            named = table[0:TOP] == (p * SIDE + j).astype(F32)
            hits.append(jnp.sum(named.astype(F32), axis=0, keepdims=True))
            scales.append(
                jnp.sum(jnp.where(named, table[8 : 8 + TOP], 0.0), axis=0, keepdims=True)
            )
        lanes = (GROUP, GROUP)
        before = (iota(lanes, 0) <= iota(lanes, 1)) & (
            iota(lanes, 0) // HERE == iota(lanes, 1) // HERE
        )
        hit = jnp.concatenate(hits + hits, axis=0)
        rank = dot(hit.astype(BF16), before.astype(BF16))
        base = (iota((1, GROUP), 1) // HERE * CAP).astype(F32) - 1.0
        number = iota((SLOTS, GROUP), 0).astype(F32)
        chosen, scaled = [], []
        for j in range(SIDE):
            slot = jnp.where(hits[j] > 0.5, base + rank[j : j + 1], -1.0)
            match = number == slot
            chosen.append(jnp.where(match, 1.0, 0.0))
            scaled.append(jnp.where(match, scales[j], 0.0))
        sel[i] = jnp.concatenate(chosen, axis=0).astype(BF16)
        spr[i] = jnp.transpose(jnp.concatenate(scaled, axis=0)).astype(BF16)

    loop(0, 2, lambda g: build(2 * g))
    wait_for(t_ret.at[:, pl.ds(0, 15 * HDIM)], a_recv.at[3])
    wait_for(s_ret.at[:, pl.ds(0, 15 * HDIM)], a_recv.at[2])
    attended = (
        tokens[...].astype(F32)
        + gate_s[...] * s_ret[...].astype(F32)
        + gate_t[...] * t_ret[...].astype(F32)
    ).astype(BF16)
    attended_out[...] = attended
    widened = attended.astype(F32)
    mean_square = jnp.mean(widened * widened, axis=-1, keepdims=True)
    tok[0, 0, c, spot] = (widened * lax.rsqrt(mean_square + 1e-06) * gain[...]).astype(BF16)

    mine, other = tok.at[0, 0, c, spot], tok.at[1, 0, c, spot]
    send(mine, other, pair_send.at[0], pair_recv.at[0], frame=at_x(2))

    def pass_on(frame, block, step, group, way):
        at = (z + block) % 4
        send(
            tok.at[frame, 0, c, at], tok.at[frame, group, c, at],
            z_send.at[frame, way], z_recv.at[frame, min(way, 3)],
            pixel=(z + step) % DEPTH * 2 + c,
        )

    def wait_block(frame, way):
        wait_for(tok.at[frame, 0, c, 0], z_recv.at[frame, way])

    def start_near(frame):
        pass_on(frame, 0, 7, 0, 0)
        pass_on(frame, 0, 1, 0, 1)

    def second_near(frame):
        wait_block(frame, 0)
        pass_on(frame, 1, 7, 0, 2)

    def start_far(frame):
        for way, (block, step) in enumerate(((2, 7), (7, 1), (2, 6), (7, 2))):
            pass_on(frame, block, step, 1, 3 + way)

    def end_near(frame):
        wait_block(frame, 1)
        wait_block(frame, 2)
        to_sibling(frame, 0)

    def to_sibling(frame, g):
        send(
            tok.at[frame, g, c], tok.at[frame, g, c],
            c_send.at[frame, g], c_recv.at[frame, g], pixel=z * 2 + 1 - c,
        )

    def dispatch(frame, g):
        i = 2 * g + frame
        wait_for(tok.at[frame, g, 1 - c], c_recv.at[frame, g])

        def columns(n):
            at = pl.ds(pl.multiple_of(n * CHUNK, CHUNK), CHUNK)
            block = tok[frame, g, :, :, :, at].reshape(GROUP, CHUNK)
            rows_out[i, :, :, at] = (
                dot(sel[i], block).astype(BF16).reshape(SIDE, SLOTS, CHUNK)
            )

        loop(0, D // CHUNK, columns)
        for step in range(1, SIDE):
            to = (y + step) % SIDE
            send(
                rows_out.at[i, to], arrive.at[i, y], y_send.at[i], y_recv.at[i], frame=at_y(to)
            )
        arrive[i, y] = rows_out[i, y]

    start_near(0)
    second_near(0)
    wait_for(other, pair_recv.at[0])
    start_near(1)
    share(2)
    share(3)
    end_near(0)
    dispatch(0, 0)
    second_near(1)
    wait_for(rt.at[1], r_recv.at[1])
    loop(0, 2, lambda g: build(2 * g + 1))
    end_near(1)
    start_far(1)
    start_far(0)
    dispatch(1, 0)

    def dispatch_far(k):
        frame = 1 - k
        wait_for(tok.at[frame, 1, c], z_recv.at[frame, 3])
        to_sibling(frame, 1)
        dispatch(frame, 1)

    loop(0, 2, dispatch_far)

    def give_back(i):
        back[i, y] = parts[i, y]
        for step in range(1, SIDE):
            to = (y + step) % SIDE
            send(parts.at[i, to], back.at[i, y], b_send.at[i], b_recv.at[i], frame=at_y(to))

    def feed_forward(i):
        wait_for(arrive.at[i, pl.ds(0, SIDE - 1)], y_recv.at[i])
        flat = arrive[i].reshape(SIDE * SLOTS, D)

        def hidden(n):
            gate = dot(flat, gu_all[pl.ds(n * GROUP, GROUP)], (1, 1))
            up = dot(flat, gu_all[pl.ds(FF_PAD + n * GROUP, GROUP)], (1, 1))
            act[n] = (jax.nn.silu(gate) * up).astype(BF16)

        loop(0, FF_PAD // GROUP, hidden)

        def columns(n):
            at = pl.ds(pl.multiple_of(n * CHUNK, CHUNK), CHUNK)
            total = dot(act[0], dn_all[0:GROUP, at])
            for m in range(1, FF_PAD // GROUP):
                total = total + dot(act[m], dn_all[m * GROUP : (m + 1) * GROUP, at])
            parts[i, :, :, at] = total.astype(BF16).reshape(SIDE, SLOTS, CHUNK)

        loop(0, D // CHUNK, columns)

    for side in range(2):
        for part in range(4):
            wait_for(dn_all.at[pl.ds(0, shares[part][-1])], w_recv.at[side, part])

    def run_experts(k):
        i = jnp.where(k < 2, k, 5 - k)
        feed_forward(i)

        @pl.when(i == 1)
        def _():
            send(parts.at[1], xin, pair_send.at[2], pair_recv.at[2], frame=at_x(2))

        @pl.when(i >= 2)
        def _():
            give_back(i)

    loop(0, 4, run_experts)
    wait_for(xin, pair_recv.at[2])

    def chunk(n):
        return pl.ds(pl.multiple_of(n * CHUNK, CHUNK), CHUNK)

    def give_back_near(n):
        at = chunk(n)
        parts[0, :, :, at] = (
            parts[0, :, :, at].astype(F32) + xin[:, :, at].astype(F32)
        ).astype(BF16)
        back[0, y, :, at] = parts[0, y, :, at]
        for step in range(1, SIDE):
            to = (y + step) % SIDE
            send(
                parts.at[0, to, :, at], back.at[0, y, :, at],
                nb_send.at[n], nb_recv.at[n], frame=at_y(to),
            )

    loop(0, D // CHUNK, give_back_near)

    def combine(k):
        i = 3 - k
        frame = i % 2
        wait_for(back.at[i, pl.ds(0, SIDE - 1)], b_recv.at[i])

        def columns(n):
            at = chunk(n)
            block = back[i, :, :, at].reshape(SIDE * SLOTS, CHUNK)
            mixed[i, :, :, :, at] = (
                dot(spr[i], block).astype(BF16).reshape(2, 4, HERE, CHUNK)
            )

        loop(0, D // CHUNK, columns)
        send(mixed.at[i, 1 - c], sib.at[i], m_send.at[i], m_recv.at[i], pixel=z * 2 + 1 - c)
        wait_for(sib.at[i], m_recv.at[i])

        def put(q):
            zred[i, q] = (mixed[i, c, q].astype(F32) + sib[i, q].astype(F32)).astype(BF16)

        loop(0, 4, put)
        for way, (block, step, side, slot) in enumerate(
            ((6, 7, 0, 0), (3, 1, 1, 0), (5, 6, 0, 1), (4, 2, 1, 1))
        ):
            send(
                zred.at[i, (z + block) % 4], zfar.at[frame, side, slot], q_send.at[frame, way],
                q_recv.at[frame], pixel=(z + step) % DEPTH * 2 + c,
            )

    loop(0, 2, combine)
    wait_for(zfar.at[1], q_recv.at[1])
    for side, block in ((1, 2), (0, 7)):
        q = (z + block) % 4
        far = zfar[1, side, 0].astype(F32) + zfar[1, side, 1].astype(F32)
        zred[1, q] = far.astype(BF16)
        send(
            zred.at[1, q], zin.at[1, side], l_send.at[side], l_recv,
            pixel=(z + block) % DEPTH * 2 + c,
        )

    def combine_near(n):
        at = chunk(n)

        @pl.when(n == D // CHUNK - 1)
        def _():
            wait_for(zin.at[1, pl.ds(0, 2)], l_recv)
            fin_out[...] = (zin[1, 0].astype(F32) + zin[1, 1].astype(F32)).astype(BF16)
            send(fin_out, fin_in, pair_send.at[1], pair_recv.at[1], frame=at_x(2))

        wait_for(back.at[0, pl.ds(0, SIDE - 1), :, at], nb_recv.at[n])
        block = back[0, :, :, at].reshape(SIDE * SLOTS, CHUNK)
        mixed[0, :, :, :, at] = dot(spr[0], block).astype(BF16).reshape(2, 4, HERE, CHUNK)
        send(
            mixed.at[0, 1 - c, :, :, at], sib.at[0, :, :, at],
            nm_send.at[n], nm_recv.at[n], pixel=z * 2 + 1 - c,
        )
        wait_for(sib.at[0, :, :, at], nm_recv.at[n])

        @pl.when(n == 0)
        def _():
            wait_for(zfar.at[0], q_recv.at[0])

        for way, block in enumerate((2, 7, 1, 0)):
            q = (z + block) % 4
            total = mixed[0, c, q, :, at].astype(F32) + sib[0, q, :, at].astype(F32)
            if way < 2:
                for slot in range(2):
                    total = total + zfar[0, 1 - way, slot, :, at].astype(F32)
            zred[0, q, :, at] = total.astype(BF16)
            if way < 3:
                send(
                    zred.at[0, q, :, at], zin.at[0, way, :, at],
                    nq_send.at[way, n], nq_recv.at[n], pixel=(z + block) % DEPTH * 2 + c,
                )

    loop(0, D // CHUNK, combine_near)
    wait_for(fin_in, pair_recv.at[1])

    def finish(n):
        at = chunk(n)
        wait_for(zin.at[0, :, :, at], nq_recv.at[n])
        result = zred[0, spot, :, at].astype(F32) + fin_in[:, at].astype(F32)
        for way in range(3):
            result = result + zin[0, way, :, at].astype(F32)
        mix_out[:, at] = result.astype(BF16)

    loop(0, D // CHUNK, finish)

    for side in range(2):
        for part in range(4):
            wait_for(dn_all.at[pl.ds(0, shares[part][-1])], w_send.at[side, part])
    wait_for(s_out.at[:, pl.ds(0, 15)], a_send.at[0])
    wait_for(t_out.at[:, pl.ds(0, 15)], a_send.at[1])
    wait_for(s_part.at[pl.ds(0, 15)], a_send.at[2])
    wait_for(t_part.at[pl.ds(0, 15)], a_send.at[3])
    wait_for(r_in.at[pl.ds(0, 15)], r_send.at[0])
    wait_for(rt.at[0], r_send.at[1])
    wait_for(mine, pair_send.at[0])
    wait_for(fin_out, pair_send.at[1])

    def sent(i):
        for frame in range(2):
            wait_for(tok.at[0, 0, 0, 0], z_send.at[frame, i])

    loop(0, 7, sent)

    def sent_far(i):
        for frame in range(2):
            wait_for(zred.at[0, 0], q_send.at[frame, i])

    loop(0, 4, sent_far)
    for side in range(2):
        wait_for(zred.at[1, 0], l_send.at[side])
    wait_for(xin, pair_send.at[2])

    def sent_groups(i):
        wait_for(tok.at[0, 0, 0], c_send.at[i % 2, i // 2])
        wait_for(rows_out.at[i, pl.ds(0, SIDE - 1)], y_send.at[i])

        @pl.when(i >= 2)
        def _():
            wait_for(parts.at[i, pl.ds(0, SIDE - 1)], b_send.at[i])
            wait_for(mixed.at[i, 0], m_send.at[i])

    loop(0, 4, sent_groups)

    def sent_chunks(n):
        at = chunk(n)
        wait_for(parts.at[0, pl.ds(0, SIDE - 1), :, at], nb_send.at[n])
        wait_for(mixed.at[0, 0, :, :, at], nm_send.at[n])
        for way in range(3):
            wait_for(zred.at[0, 0, :, at], nq_send.at[way, n])

    loop(0, D // CHUNK, sent_chunks)


def per_device(
    tokens,
    spatial_inputs,
    temporal_inputs,
    gate_spatial,
    gate_temporal,
    norm_gain,
    route_experts,
    route_weights,
    expert_gate_up,
    expert_down,
):
    vmem = pl.BlockSpec(memory_space=pltpu.VMEM)
    hbm = pl.BlockSpec(memory_space=pl.ANY)
    dma = pltpu.SemaphoreType.DMA

    def buf(*shape, dtype=BF16):
        return pltpu.VMEM(shape, dtype)

    attended, mix = pl.pallas_call(
        kernel,
        out_shape=[jax.ShapeDtypeStruct((HERE, D), BF16)] * 2,
        in_specs=[hbm] * 3 + [vmem] * 5 + [hbm] * 2,
        out_specs=[vmem] * 2,
        scratch_shapes=[
            buf(HERE, D), buf(HERE, 3 * D), buf(HERE, 3 * D),
            buf(2 * FF_PAD, D), buf(FF_PAD, D), buf(FF_PAD // GROUP, GROUP, GROUP),
            buf(3, HEADS, HERE, HDIM), buf(3, HEADS, HERE, HDIM),
            buf(3, HEADS, HERE, HDIM), buf(3, HEADS, HERE, HDIM),
            buf(HEADS, HERE, HDIM), buf(HEADS, HERE, HDIM), buf(HERE, D), buf(HERE, D),
            buf(16, 128), buf(16, 16, 128), buf(2, 2, 2, 16, 128),
            buf(2, 2, 2, 4, HERE, D),
            buf(4, GROUP, GROUP), buf(4, GROUP, GROUP),
            buf(4, SIDE, SLOTS, D), buf(4, SIDE, SLOTS, D), buf(4, SIDE, SLOTS, D),
            buf(4, SIDE, SLOTS, D),
            buf(4, 2, 4, HERE, D), buf(4, 4, HERE, D), buf(4, 4, HERE, D),
            buf(2, 3, HERE, D), buf(2, 2, 2, HERE, D),
            buf(HERE, D), buf(HERE, D), buf(SIDE, SLOTS, D),
            dma((6,)), dma((2, 4)), dma((2, 4)), dma((4,)), dma((4,)), dma((2,)), dma((2,)),
            dma((3,)), dma((3,)), dma((2, 7)), dma((2, 4)), dma((2, 2)), dma((2, 2)),
            dma((4,)), dma((4,)), dma((4,)), dma((4,)), dma((4,)), dma((4,)),
            dma((2, 4)), dma((2,)), dma((2,)), dma(()), dma((4,)), dma((4,)), dma((4,)), dma((4,)),
            dma((3, 4)), dma((4,)),
        ],
        compiler_params=pltpu.CompilerParams(
            collective_id=0, has_side_effects=True, vmem_limit_bytes=60 * 1024 * 1024
        ),
    )(
        tokens[0],
        spatial_inputs[0],
        temporal_inputs[0],
        gate_spatial[None],
        gate_temporal[None],
        norm_gain[None],
        jnp.transpose(route_experts, (2, 0, 1)),
        jnp.transpose(route_weights, (2, 0, 1)),
        jnp.transpose(expert_gate_up, (0, 2, 1))[0],
        expert_down[0],
    )
    return (attended[None], mix[None])


def solution(mesh):
    in_specs = (
        P("frame", "pixel", None),
        P("frame", "pixel", None),
        P("frame", "pixel", None),
        P(),
        P(),
        P(),
        P("frame", "pixel", None),
        P("frame", "pixel", None),
        P(("frame", "pixel"), None, None),
        P(("frame", "pixel"), None, None),
    )
    out_specs = (P("frame", "pixel", None), P("frame", "pixel", None))
    return jax.shard_map(
        per_device, mesh=mesh, in_specs=in_specs, out_specs=out_specs, check_vma=False
    )
```

time: 203 us -> 147 us (0.72)
  Pallas kernels: 199 us -> 143 us
    pallas_call x1, Pallas kernels: 199 us -> 143 us  [per_device(): pl.pallas_call(kernel, out_shape=[jax.ShapeDtypeStruct((HERE, D), BF16)]...]
where the time goes in v5:
time: 147 us; the launch traced here: 146 us
  Pallas kernels  143 us (97%)
  local copies, waits for them, and re-layouts  3.14 us (2%)
    pallas_call x1, Pallas kernels, per_device(): pl.pallas_call(kernel, out_shape=[jax.ShapeDtypeStruct((HERE, D), BF16)]...  143 us
    unnamed x2, local copies, waits for them, and re-layouts  3.14 us

profile of v5, /device:TPU:1, one launch (start us, length us, event | category | flops | bytes accessed | tf_op | source)
XLA Modules:
  0.0 146.4 jit_solution(12382652416301024169)
XLA Ops:
  0.6 142.6 %shard_map.113 = (bf16[32,2048]{1,0:T(8,128)(2,1)}, bf16[32,2048]{1,0:T(8,128)(2,1)}) custom-call(bf16[32,2048]{1,0:T(8,128)(2,1)} %bitcast.18, bf16[32,6144]{1,0:T(8,128)(2,1)} %bitcast.16, bf16[32,6144]{1,0:T(8,128)(2,1)} %bitcast.17, f32[1,2048]{1,0:T(1,128)} %bitcast.21, f32[1,2048]{1,0:T(1,128)} %bitcast.22, f32[1,2048]{1,0:T(1,128)} %bitcast.23, ...), custom_call_target="tpu_custom_call" | custom-call | tf_op jit(solution)/shard_map/pallas_call | solution.py:555
  143.2 1.6 %copy.14 = bf16[1,32,2048]{2,1,0:T(8,128)(2,1)} copy(bf16[1,32,2048]{2,1,0:T(8,128)(2,1)} %bitcast.20) | data formatting | bytes 262144
  144.8 1.6 %copy.15 = bf16[1,32,2048]{2,1,0:T(8,128)(2,1)} copy(bf16[1,32,2048]{2,1,0:T(8,128)(2,1)} %bitcast.19) | data formatting | bytes 262144

commit v6 on v5

--- a/solution.py
+++ b/solution.py
@@ -76,14 +76,14 @@
 
 def kernel(
     tokens_in, spatial_in, temporal_in, gate_s, gate_t, gain, experts, weights, gate_up, down,
-    attended_out, mix_out,
+    out,
     tokens, spatial, temporal, gu_all, dn_all, act,
     s_out, s_in, t_out, t_in, s_part, t_part, s_ret, t_ret,
     r_out, r_in, rt, tok, sel, spr, rows_out, arrive, parts, back, mixed, sib, zred, zin,
-    zfar, fin_out, fin_in, xin,
+    zfar, xfar, xin,
     load_sem, w_send, w_recv, a_send, a_recv, r_send, r_recv, pair_send, pair_recv,
     z_send, z_recv, c_send, c_recv, y_send, y_recv, b_send, b_recv, m_send, m_recv,
-    q_send, q_recv, l_send, l_recv, nb_send, nb_recv, nm_send, nm_recv, nq_send, nq_recv,
+    q_send, q_recv, f_send, f_recv, nq_send, nq_recv,
 ):
     f = lax.axis_index("frame")
     p = lax.axis_index("pixel")
@@ -167,6 +167,7 @@
 
     wait_for(t_in.at[:, pl.ds(0, 15)], a_recv.at[1])
 
+
     attend(t_in, t_part, True)
 
     def return_t(i):
@@ -186,6 +187,7 @@
         send(r_out, r_in.at[p], r_send.at[0], r_recv.at[0], pixel=(p + i) % 16)
 
     loop(1, 16, scatter_routes)
+
     attend(s_in, s_part, False)
 
     def return_s(i):
@@ -250,7 +252,7 @@
         + gate_s[...] * s_ret[...].astype(F32)
         + gate_t[...] * t_ret[...].astype(F32)
     ).astype(BF16)
-    attended_out[...] = attended
+    out[0] = attended
     widened = attended.astype(F32)
     mean_square = jnp.mean(widened * widened, axis=-1, keepdims=True)
     tok[0, 0, c, spot] = (widened * lax.rsqrt(mean_square + 1e-06) * gain[...]).astype(BF16)
@@ -258,33 +260,22 @@
     mine, other = tok.at[0, 0, c, spot], tok.at[1, 0, c, spot]
     send(mine, other, pair_send.at[0], pair_recv.at[0], frame=at_x(2))
 
-    def pass_on(frame, block, step, group, way):
-        at = (z + block) % 4
+    def home(d):
+        return 0 if -1 <= d <= 2 else 1
+
+    def pass_on(frame, d, step):
+        at, there = (z + d) % 4, d - step
+        if there == -4:
+            there = 4
         send(
-            tok.at[frame, 0, c, at], tok.at[frame, group, c, at],
-            z_send.at[frame, way], z_recv.at[frame, min(way, 3)],
+            tok.at[frame, home(d), c, at], tok.at[frame, home(there), c, at],
+            z_send.at[frame, there + 3], z_recv.at[frame, there + 3],
             pixel=(z + step) % DEPTH * 2 + c,
         )
 
-    def wait_block(frame, way):
-        wait_for(tok.at[frame, 0, c, 0], z_recv.at[frame, way])
-
-    def start_near(frame):
-        pass_on(frame, 0, 7, 0, 0)
-        pass_on(frame, 0, 1, 0, 1)
-
-    def second_near(frame):
-        wait_block(frame, 0)
-        pass_on(frame, 1, 7, 0, 2)
-
-    def start_far(frame):
-        for way, (block, step) in enumerate(((2, 7), (7, 1), (2, 6), (7, 2))):
-            pass_on(frame, block, step, 1, 3 + way)
-
-    def end_near(frame):
-        wait_block(frame, 1)
-        wait_block(frame, 2)
-        to_sibling(frame, 0)
+    def got(frame, *blocks):
+        for d in blocks:
+            wait_for(tok.at[frame, home(d), c, 0], z_recv.at[frame, d + 3])
 
     def to_sibling(frame, g):
         send(
@@ -303,7 +294,8 @@
                 dot(sel[i], block).astype(BF16).reshape(SIDE, SLOTS, CHUNK)
             )
 
-        loop(0, D // CHUNK, columns)
+        for n in range(D // CHUNK):
+            columns(n)
         for step in range(1, SIDE):
             to = (y + step) % SIDE
             send(
@@ -311,38 +303,94 @@
             )
         arrive[i, y] = rows_out[i, y]
 
-    start_near(0)
-    second_near(0)
+    pass_on(0, 0, -1)
+    pass_on(0, 0, 1)
+    got(0, 1, -1)
+    pass_on(0, 1, -1)
+    pass_on(0, -1, 1)
     wait_for(other, pair_recv.at[0])
-    start_near(1)
+    pass_on(1, 0, -1)
+    pass_on(1, 0, 1)
     share(2)
     share(3)
-    end_near(0)
+    got(0, 2, -2)
+    to_sibling(0, 0)
+    pass_on(0, 2, -1)
+    pass_on(0, -2, 1)
+    got(1, 1, -1)
+    pass_on(1, 1, -1)
+
+    @pl.when(c == 1)
+    def _():
+        pass_on(1, -1, 1)
+
     dispatch(0, 0)
-    second_near(1)
+    got(0, 3, -3)
+    pass_on(0, 3, -1)
     wait_for(rt.at[1], r_recv.at[1])
     loop(0, 2, lambda g: build(2 * g + 1))
-    end_near(1)
-    start_far(1)
-    start_far(0)
+    got(1, 2)
+    to_sibling(1, 0)
+
+    @pl.when(c == 1)
+    def _():
+        got(1, -2)
+        pass_on(1, 2, -1)
+        pass_on(1, -2, 1)
+
+    got(0, 4)
+    to_sibling(0, 1)
+    dispatch(0, 1)
+
+    @pl.when(c == 1)
+    def _():
+        got(1, 3, -3)
+        pass_on(1, -3, 1)
+
     dispatch(1, 0)
 
-    def dispatch_far(k):
-        frame = 1 - k
-        wait_for(tok.at[frame, 1, c], z_recv.at[frame, 3])
-        to_sibling(frame, 1)
-        dispatch(frame, 1)
-
-    loop(0, 2, dispatch_far)
-
-    def give_back(i):
-        back[i, y] = parts[i, y]
+    @pl.when(c == 1)
+    def _():
+        got(1, 4)
+        to_sibling(1, 1)
+
+    @pl.when(c == 0)
+    def _():
+        wait_for(tok.at[1, 1, 1], c_recv.at[1, 1])
+
+    low, high = pl.ds(0, SLOTS // 2), pl.ds(SLOTS // 2, SLOTS // 2)
+    chosen = sel[3, :, GROUP // 2 :].reshape(SIDE, SLOTS, GROUP // 2)[:, SLOTS // 2 :]
+    chosen = chosen.reshape(SIDE * SLOTS // 2, GROUP // 2)
+    for n in range(D // CHUNK):
+        at = pl.ds(n * CHUNK, CHUNK)
+        block = tok[1, 1, 1, :, :, at].reshape(GROUP // 2, CHUNK)
+        rows_out[3, :, high, at] = (
+            dot(chosen, block).astype(BF16).reshape(SIDE, SLOTS // 2, CHUNK)
+        )
+    for step in range(1, SIDE):
+        to = (y + step) % SIDE
+        send(
+            rows_out.at[3, to, high], arrive.at[3, y, high], y_send.at[3], y_recv.at[3],
+            frame=at_y(to),
+        )
+    arrive[3, y, high] = rows_out[3, y, high]
+    wait_for(arrive.at[2, pl.ds(0, SIDE - 1)], y_recv.at[2])
+    send(arrive.at[2, :, low], arrive.at[3, :, low], pair_send.at[3], pair_recv.at[3], frame=at_x(2))
+
+    def chunk(n):
+        return pl.ds(pl.multiple_of(n * CHUNK, CHUNK), CHUNK)
+
+    def give_back(i, n):
+        at = chunk(n)
+        back[i, y, :, at] = parts[i, y, :, at]
         for step in range(1, SIDE):
             to = (y + step) % SIDE
-            send(parts.at[i, to], back.at[i, y], b_send.at[i], b_recv.at[i], frame=at_y(to))
+            send(
+                parts.at[i, to, :, at], back.at[i, y, :, at],
+                b_send.at[i, n], b_recv.at[i, n], frame=at_y(to),
+            )
 
     def feed_forward(i):
-        wait_for(arrive.at[i, pl.ds(0, SIDE - 1)], y_recv.at[i])
         flat = arrive[i].reshape(SIDE * SLOTS, D)
 
         def hidden(n):
@@ -350,7 +398,8 @@
             up = dot(flat, gu_all[pl.ds(FF_PAD + n * GROUP, GROUP)], (1, 1))
             act[n] = (jax.nn.silu(gate) * up).astype(BF16)
 
-        loop(0, FF_PAD // GROUP, hidden)
+        for n in range(FF_PAD // GROUP):
+            hidden(n)
 
         def columns(n):
             at = pl.ds(pl.multiple_of(n * CHUNK, CHUNK), CHUNK)
@@ -359,131 +408,105 @@
                 total = total + dot(act[m], dn_all[m * GROUP : (m + 1) * GROUP, at])
             parts[i, :, :, at] = total.astype(BF16).reshape(SIDE, SLOTS, CHUNK)
 
-        loop(0, D // CHUNK, columns)
+            @pl.when((i == 3) | ((i == 2) & (n < 2)))
+            def _():
+                give_back(i, n)
+
+        for n in range(D // CHUNK):
+            columns(n)
 
     for side in range(2):
         for part in range(4):
             wait_for(dn_all.at[pl.ds(0, shares[part][-1])], w_recv.at[side, part])
 
     def run_experts(k):
-        i = jnp.where(k < 2, k, 5 - k)
+        i = k % 2 * 2 + k // 2
+
+        @pl.when(i < 2)
+        def _():
+            wait_for(arrive.at[i, pl.ds(0, SIDE - 1)], y_recv.at[i])
+
+        @pl.when(i == 3)
+        def _():
+            wait_for(arrive.at[3, pl.ds(0, SIDE - 1), high], y_recv.at[3])
+            wait_for(arrive.at[3, :, low], pair_recv.at[3])
+
         feed_forward(i)
 
         @pl.when(i == 1)
         def _():
             send(parts.at[1], xin, pair_send.at[2], pair_recv.at[2], frame=at_x(2))
 
-        @pl.when(i >= 2)
-        def _():
-            give_back(i)
-
     loop(0, 4, run_experts)
-    wait_for(xin, pair_recv.at[2])
-
-    def chunk(n):
-        return pl.ds(pl.multiple_of(n * CHUNK, CHUNK), CHUNK)
-
+    loop(2, 4, lambda n: give_back(2, n))
     def give_back_near(n):
         at = chunk(n)
         parts[0, :, :, at] = (
             parts[0, :, :, at].astype(F32) + xin[:, :, at].astype(F32)
         ).astype(BF16)
-        back[0, y, :, at] = parts[0, y, :, at]
-        for step in range(1, SIDE):
-            to = (y + step) % SIDE
+        give_back(0, n)
+
+    def combine(i, n):
+        at = chunk(n)
+        wait_for(back.at[i, pl.ds(0, SIDE - 1), :, at], b_recv.at[i, n])
+        block = back[i, :, :, at].reshape(SIDE * SLOTS, CHUNK)
+        mixed[i, :, :, :, at] = dot(spr[i], block).astype(BF16).reshape(2, 4, HERE, CHUNK)
+        send(
+            mixed.at[i, 1 - c, :, :, at], sib.at[i, :, :, at],
+            m_send.at[i, n], m_recv.at[i, n], pixel=z * 2 + 1 - c,
+        )
+
+    def summed(i, q, at):
+        return mixed[i, c, q, :, at].astype(F32) + sib[i, q, :, at].astype(F32)
+
+    def partner_far(n):
+        at = chunk(n)
+        combine(3, n)
+        wait_for(sib.at[3, :, :, at], m_recv.at[3, n])
+        for q in range(4):
+            zred[3, q, :, at] = summed(3, q, at).astype(BF16)
+        send(
+            zred.at[3, :, :, at], xfar.at[:, :, at], f_send.at[n], f_recv.at[n], frame=at_x(2)
+        )
+
+    def own_far(n):
+        at = chunk(n)
+        wait_for(sib.at[2, :, :, at], m_recv.at[2, n])
+        wait_for(xfar.at[:, :, at], f_recv.at[n])
+        for way, (block, step, side, slot) in enumerate(
+            ((5, 6, 0, 1), (4, 2, 1, 1), (6, 7, 0, 0), (3, 1, 1, 0))
+        ):
+            q = (z + block) % 4
+            zred[2, q, :, at] = (summed(2, q, at) + xfar[q, :, at].astype(F32)).astype(BF16)
             send(
-                parts.at[0, to, :, at], back.at[0, y, :, at],
-                nb_send.at[n], nb_recv.at[n], frame=at_y(to),
+                zred.at[2, q, :, at], zfar.at[side, slot, :, at], q_send.at[way, n], q_recv.at[n],
+                pixel=(z + step) % DEPTH * 2 + c,
             )
 
-    loop(0, D // CHUNK, give_back_near)
-
-    def combine(k):
-        i = 3 - k
-        frame = i % 2
-        wait_for(back.at[i, pl.ds(0, SIDE - 1)], b_recv.at[i])
-
-        def columns(n):
-            at = chunk(n)
-            block = back[i, :, :, at].reshape(SIDE * SLOTS, CHUNK)
-            mixed[i, :, :, :, at] = (
-                dot(spr[i], block).astype(BF16).reshape(2, 4, HERE, CHUNK)
-            )
-
-        loop(0, D // CHUNK, columns)
-        send(mixed.at[i, 1 - c], sib.at[i], m_send.at[i], m_recv.at[i], pixel=z * 2 + 1 - c)
-        wait_for(sib.at[i], m_recv.at[i])
-
-        def put(q):
-            zred[i, q] = (mixed[i, c, q].astype(F32) + sib[i, q].astype(F32)).astype(BF16)
-
-        loop(0, 4, put)
-        for way, (block, step, side, slot) in enumerate(
-            ((6, 7, 0, 0), (3, 1, 1, 0), (5, 6, 0, 1), (4, 2, 1, 1))
-        ):
-            send(
-                zred.at[i, (z + block) % 4], zfar.at[frame, side, slot], q_send.at[frame, way],
-                q_recv.at[frame], pixel=(z + step) % DEPTH * 2 + c,
-            )
-
-    loop(0, 2, combine)
-    wait_for(zfar.at[1], q_recv.at[1])
-    for side, block in ((1, 2), (0, 7)):
-        q = (z + block) % 4
-        far = zfar[1, side, 0].astype(F32) + zfar[1, side, 1].astype(F32)
-        zred[1, q] = far.astype(BF16)
-        send(
-            zred.at[1, q], zin.at[1, side], l_send.at[side], l_recv,
-            pixel=(z + block) % DEPTH * 2 + c,
-        )
-
-    def combine_near(n):
-        at = chunk(n)
-
-        @pl.when(n == D // CHUNK - 1)
-        def _():
-            wait_for(zin.at[1, pl.ds(0, 2)], l_recv)
-            fin_out[...] = (zin[1, 0].astype(F32) + zin[1, 1].astype(F32)).astype(BF16)
-            send(fin_out, fin_in, pair_send.at[1], pair_recv.at[1], frame=at_x(2))
-
-        wait_for(back.at[0, pl.ds(0, SIDE - 1), :, at], nb_recv.at[n])
-        block = back[0, :, :, at].reshape(SIDE * SLOTS, CHUNK)
-        mixed[0, :, :, :, at] = dot(spr[0], block).astype(BF16).reshape(2, 4, HERE, CHUNK)
-        send(
-            mixed.at[0, 1 - c, :, :, at], sib.at[0, :, :, at],
-            nm_send.at[n], nm_recv.at[n], pixel=z * 2 + 1 - c,
-        )
-        wait_for(sib.at[0, :, :, at], nm_recv.at[n])
-
-        @pl.when(n == 0)
-        def _():
-            wait_for(zfar.at[0], q_recv.at[0])
-
+    def own_near(n):
+        at = chunk(n)
+        wait_for(sib.at[0, :, :, at], m_recv.at[0, n])
+        wait_for(zfar.at[:, :, :, at], q_recv.at[n])
         for way, block in enumerate((2, 7, 1, 0)):
             q = (z + block) % 4
-            total = mixed[0, c, q, :, at].astype(F32) + sib[0, q, :, at].astype(F32)
+            total = summed(0, q, at)
             if way < 2:
                 for slot in range(2):
-                    total = total + zfar[0, 1 - way, slot, :, at].astype(F32)
+                    total = total + zfar[1 - way, slot, :, at].astype(F32)
             zred[0, q, :, at] = total.astype(BF16)
             if way < 3:
                 send(
-                    zred.at[0, q, :, at], zin.at[0, way, :, at],
+                    zred.at[0, q, :, at], zin.at[way, :, at],
                     nq_send.at[way, n], nq_recv.at[n], pixel=(z + block) % DEPTH * 2 + c,
                 )
 
-    loop(0, D // CHUNK, combine_near)
-    wait_for(fin_in, pair_recv.at[1])
-
-    def finish(n):
-        at = chunk(n)
-        wait_for(zin.at[0, :, :, at], nq_recv.at[n])
-        result = zred[0, spot, :, at].astype(F32) + fin_in[:, at].astype(F32)
-        for way in range(3):
-            result = result + zin[0, way, :, at].astype(F32)
-        mix_out[:, at] = result.astype(BF16)
-
-    loop(0, D // CHUNK, finish)
+    loop(0, 2, lambda n: combine(2, n))
+    loop(0, 4, partner_far)
+    wait_for(xin, pair_recv.at[2])
+    loop(0, 4, give_back_near)
+    loop(2, 4, lambda n: combine(2, n))
+
+    loop(0, 3, own_far)
 
     for side in range(2):
         for part in range(4):
@@ -495,40 +518,66 @@
     wait_for(r_in.at[pl.ds(0, 15)], r_send.at[0])
     wait_for(rt.at[0], r_send.at[1])
     wait_for(mine, pair_send.at[0])
-    wait_for(fin_out, pair_send.at[1])
-
-    def sent(i):
-        for frame in range(2):
-            wait_for(tok.at[0, 0, 0, 0], z_send.at[frame, i])
-
-    loop(0, 7, sent)
-
-    def sent_far(i):
-        for frame in range(2):
-            wait_for(zred.at[0, 0], q_send.at[frame, i])
-
-    loop(0, 4, sent_far)
-    for side in range(2):
-        wait_for(zred.at[1, 0], l_send.at[side])
+
+    def sent(frame, *blocks):
+        for d in blocks:
+            wait_for(tok.at[0, 0, 0, 0], z_send.at[frame, d + 3])
+
+    sent(0, -3, -2, -1, 1, 2, 3, 4)
+    sent(1, -1, 1, 2)
+
+    @pl.when(c == 1)
+    def _():
+        sent(1, -3, -2, 3, 4)
+        wait_for(tok.at[0, 0, 0], c_send.at[1, 1])
+
     wait_for(xin, pair_send.at[2])
 
     def sent_groups(i):
         wait_for(tok.at[0, 0, 0], c_send.at[i % 2, i // 2])
         wait_for(rows_out.at[i, pl.ds(0, SIDE - 1)], y_send.at[i])
 
-        @pl.when(i >= 2)
+    loop(0, 3, sent_groups)
+    wait_for(rows_out.at[3, pl.ds(0, SIDE - 1), high], y_send.at[3])
+    wait_for(arrive.at[3, :, low], pair_send.at[3])
+
+    def sent_parts(n):
+        at = chunk(n)
+        for i in (2, 3):
+            wait_for(parts.at[i, pl.ds(0, SIDE - 1), :, at], b_send.at[i, n])
+
+    loop(0, D // CHUNK, sent_parts)
+
+    def last_steps(n):
+        combine(0, n)
+        own_near(n)
+
+        @pl.when(n == 0)
         def _():
-            wait_for(parts.at[i, pl.ds(0, SIDE - 1)], b_send.at[i])
-            wait_for(mixed.at[i, 0], m_send.at[i])
-
-    loop(0, 4, sent_groups)
+            own_far(3)
+
+    loop(0, 4, last_steps)
+
+    def finish(n):
+        at = chunk(n)
+        wait_for(zin.at[:, :, at], nq_recv.at[n])
+        result = zred[0, spot, :, at].astype(F32)
+        for way in range(3):
+            result = result + zin[way, :, at].astype(F32)
+        out[1, :, at] = result.astype(BF16)
+
+    loop(0, 4, finish)
 
     def sent_chunks(n):
         at = chunk(n)
-        wait_for(parts.at[0, pl.ds(0, SIDE - 1), :, at], nb_send.at[n])
-        wait_for(mixed.at[0, 0, :, :, at], nm_send.at[n])
+        for i in (0, 2, 3):
+            wait_for(mixed.at[i, 0, :, :, at], m_send.at[i, n])
+        wait_for(parts.at[0, pl.ds(0, SIDE - 1), :, at], b_send.at[0, n])
         for way in range(3):
             wait_for(zred.at[0, 0, :, at], nq_send.at[way, n])
+        for way in range(4):
+            wait_for(zred.at[0, 0, :, at], q_send.at[way, n])
+        wait_for(zred.at[3, :, :, at], f_send.at[n])
 
     loop(0, D // CHUNK, sent_chunks)
 
@@ -552,11 +601,11 @@
     def buf(*shape, dtype=BF16):
         return pltpu.VMEM(shape, dtype)
 
-    attended, mix = pl.pallas_call(
+    both = pl.pallas_call(
         kernel,
-        out_shape=[jax.ShapeDtypeStruct((HERE, D), BF16)] * 2,
+        out_shape=jax.ShapeDtypeStruct((2, HERE, D), BF16),
         in_specs=[hbm] * 3 + [vmem] * 5 + [hbm] * 2,
-        out_specs=[vmem] * 2,
+        out_specs=vmem,
         scratch_shapes=[
             buf(HERE, D), buf(HERE, 3 * D), buf(HERE, 3 * D),
             buf(2 * FF_PAD, D), buf(FF_PAD, D), buf(FF_PAD // GROUP, GROUP, GROUP),
@@ -569,13 +618,12 @@
             buf(4, SIDE, SLOTS, D), buf(4, SIDE, SLOTS, D), buf(4, SIDE, SLOTS, D),
             buf(4, SIDE, SLOTS, D),
             buf(4, 2, 4, HERE, D), buf(4, 4, HERE, D), buf(4, 4, HERE, D),
-            buf(2, 3, HERE, D), buf(2, 2, 2, HERE, D),
-            buf(HERE, D), buf(HERE, D), buf(SIDE, SLOTS, D),
+            buf(3, HERE, D), buf(2, 2, HERE, D), buf(4, HERE, D),
+            buf(SIDE, SLOTS, D),
             dma((6,)), dma((2, 4)), dma((2, 4)), dma((4,)), dma((4,)), dma((2,)), dma((2,)),
-            dma((3,)), dma((3,)), dma((2, 7)), dma((2, 4)), dma((2, 2)), dma((2, 2)),
-            dma((4,)), dma((4,)), dma((4,)), dma((4,)), dma((4,)), dma((4,)),
-            dma((2, 4)), dma((2,)), dma((2,)), dma(()), dma((4,)), dma((4,)), dma((4,)), dma((4,)),
-            dma((3, 4)), dma((4,)),
+            dma((4,)), dma((4,)), dma((2, 8)), dma((2, 8)), dma((2, 2)), dma((2, 2)),
+            dma((4,)), dma((4,)), dma((4, 4)), dma((4, 4)), dma((4, 4)), dma((4, 4)),
+            dma((4, 4)), dma((4,)), dma((4,)), dma((4,)), dma((3, 4)), dma((4,)),
         ],
         compiler_params=pltpu.CompilerParams(
             collective_id=0, has_side_effects=True, vmem_limit_bytes=60 * 1024 * 1024
@@ -592,7 +640,7 @@
         jnp.transpose(expert_gate_up, (0, 2, 1))[0],
         expert_down[0],
     )
-    return (attended[None], mix[None])
+    return (both[:1], both[1:])
 
 
 def solution(mesh):

time: 147 us -> 137 us (0.932)
  Pallas kernels: 143 us -> 135 us
    pallas_call x1, Pallas kernels: 143 us -> 135 us  [per_device(): pl.pallas_call(kernel, out_shape=jax.ShapeDtypeStruct((2, HERE, D), BF16)...]
    unnamed x2 -> x0, local copies, waits for them, and re-layouts: 3.14 us -> none
    slice x0 -> x1, local copies, waits for them, and re-layouts: none -> 1.68 us  [per_device(): return (both[:1], both[1:])]
where the time goes in v6:
time: 137 us
  Pallas kernels  135 us (99%)
  local copies, waits for them, and re-layouts  1.68 us (1%)
    pallas_call x1, Pallas kernels, per_device(): pl.pallas_call(kernel, out_shape=jax.ShapeDtypeStruct((2, HERE, D), BF16)...  135 us

profile of v6, /device:TPU:1, one launch (start us, length us, event | category | flops | bytes accessed | tf_op | source)
XLA Modules:
  0.0 137.1 jit_solution(16558130940525674731)
XLA Ops:
  0.6 134.7 %shard_map.113 = bf16[2,32,2048]{2,1,0:T(8,128)(2,1)} custom-call(bf16[32,2048]{1,0:T(8,128)(2,1)} %bitcast.16, bf16[32,6144]{1,0:T(8,128)(2,1)} %bitcast.14, bf16[32,6144]{1,0:T(8,128)(2,1)} %bitcast.15, f32[1,2048]{1,0:T(1,128)} %bitcast.17, f32[1,2048]{1,0:T(1,128)} %bitcast.18, f32[1,2048]{1,0:T(1,128)} %bitcast.19, s32[6,1,32]{2,1,0:T(1,128)} %bitcast.20, ...), custom_call_target="tpu_custom_call" | custom-call | tf_op jit(solution)/shard_map/pallas_call | solution.py:604
  135.4 1.7 %fusion = (bf16[1,32,2048]{2,1,0:T(8,128)(2,1)}, bf16[1,32,2048]{2,1,0:T(8,128)(2,1)}) fusion(bf16[2,32,2048]{2,1,0:T(8,128)(2,1)} %shard_map.113), kind=kLoop, calls=%fused_computation | loop fusion | bytes 524288 | tf_op jit(solution)/shard_map/slice | solution.py:643

commit v7 on v6

--- a/solution.py
+++ b/solution.py
@@ -83,7 +83,7 @@
     zfar, xfar, xin,
     load_sem, w_send, w_recv, a_send, a_recv, r_send, r_recv, pair_send, pair_recv,
     z_send, z_recv, c_send, c_recv, y_send, y_recv, b_send, b_recv, m_send, m_recv,
-    q_send, q_recv, f_send, f_recv, nq_send, nq_recv,
+    q_send, q_recv, f_send, f_recv, h_send, h_recv, nq_send, nq_recv,
 ):
     f = lax.axis_index("frame")
     p = lax.axis_index("pixel")
@@ -138,10 +138,13 @@
 
     pl.semaphore_wait(barrier, 30)
 
-    def scatter_heads(i):
-        to_f, to_p = (f + i) % 16, (p + i) % 16
+    def peer(k):
+        return jnp.where(k % 2 == 1, 8 - k // 2, 8 + k // 2)
+
+    def scatter_heads(k):
+        to_f, to_p = (f + peer(k)) % 16, (p + peer(k)) % 16
+        send(s_out.at[:, to_p], s_in.at[:, p], a_send.at[0], a_recv.at[0], pixel=to_p)
         send(t_out.at[:, to_f], t_in.at[:, f], a_send.at[1], a_recv.at[1], frame=to_f)
-        send(s_out.at[:, to_p], s_in.at[:, p], a_send.at[0], a_recv.at[0], pixel=to_p)
 
     loop(1, 16, scatter_heads)
 
@@ -190,8 +193,8 @@
 
     attend(s_in, s_part, False)
 
-    def return_s(i):
-        to = (p + i) % 16
+    def return_s(k):
+        to = (p + peer(k)) % 16
         send(
             s_part.at[to], s_ret.at[:, pl.ds(pl.multiple_of(p * HDIM, HDIM), HDIM)],
             a_send.at[2], a_recv.at[2], pixel=to,
@@ -244,7 +247,6 @@
         sel[i] = jnp.concatenate(chosen, axis=0).astype(BF16)
         spr[i] = jnp.transpose(jnp.concatenate(scaled, axis=0)).astype(BF16)
 
-    loop(0, 2, lambda g: build(2 * g))
     wait_for(t_ret.at[:, pl.ds(0, 15 * HDIM)], a_recv.at[3])
     wait_for(s_ret.at[:, pl.ds(0, 15 * HDIM)], a_recv.at[2])
     attended = (
@@ -305,8 +307,9 @@
 
     pass_on(0, 0, -1)
     pass_on(0, 0, 1)
+    pass_on(0, 0, -2)
+    loop(0, 2, lambda g: build(2 * g))
     got(0, 1, -1)
-    pass_on(0, 1, -1)
     pass_on(0, -1, 1)
     wait_for(other, pair_recv.at[0])
     pass_on(1, 0, -1)
@@ -383,7 +386,7 @@
     def give_back(i, n):
         at = chunk(n)
         back[i, y, :, at] = parts[i, y, :, at]
-        for step in range(1, SIDE):
+        for step in (2, 1, 3):
             to = (y + step) % SIDE
             send(
                 parts.at[i, to, :, at], back.at[i, y, :, at],
@@ -408,7 +411,14 @@
                 total = total + dot(act[m], dn_all[m * GROUP : (m + 1) * GROUP, at])
             parts[i, :, :, at] = total.astype(BF16).reshape(SIDE, SLOTS, CHUNK)
 
-            @pl.when((i == 3) | ((i == 2) & (n < 2)))
+            @pl.when(i == 1)
+            def _():
+                send(
+                    parts.at[1, :, :, at], xin.at[:, :, at], h_send.at[n], h_recv.at[n],
+                    frame=at_x(2),
+                )
+
+            @pl.when(((i == 3) & (n < 1)) | ((i == 2) & (n < 2)))
             def _():
                 give_back(i, n)
 
@@ -433,18 +443,24 @@
 
         feed_forward(i)
 
-        @pl.when(i == 1)
+
+    loop(0, 4, run_experts)
+    def issue(k):
+        late = (k >= 2) & (k < 6)
+        i = jnp.where(late, 3, jnp.where(k < 8, 2, 0))
+        n = jnp.where(late, k - 2, jnp.where(k < 2, k, jnp.where(k < 8, k - 4, k - 8)))
+        at = chunk(n)
+
+        @pl.when((k >= 8) & (k < 12))
         def _():
-            send(parts.at[1], xin, pair_send.at[2], pair_recv.at[2], frame=at_x(2))
-
-    loop(0, 4, run_experts)
-    loop(2, 4, lambda n: give_back(2, n))
-    def give_back_near(n):
-        at = chunk(n)
-        parts[0, :, :, at] = (
-            parts[0, :, :, at].astype(F32) + xin[:, :, at].astype(F32)
-        ).astype(BF16)
-        give_back(0, n)
+            wait_for(xin.at[:, :, at], h_recv.at[n])
+            parts[0, :, :, at] = (
+                parts[0, :, :, at].astype(F32) + xin[:, :, at].astype(F32)
+            ).astype(BF16)
+
+        @pl.when(k < 12)
+        def _():
+            give_back(i, n)
 
     def combine(i, n):
         at = chunk(n)
@@ -461,6 +477,7 @@
 
     def partner_far(n):
         at = chunk(n)
+        issue(n + 5)
         combine(3, n)
         wait_for(sib.at[3, :, :, at], m_recv.at[3, n])
         for q in range(4):
@@ -500,11 +517,18 @@
                     nq_send.at[way, n], nq_recv.at[n], pixel=(z + block) % DEPTH * 2 + c,
                 )
 
-    loop(0, 2, lambda n: combine(2, n))
+    def first_far(n):
+        issue(n + 3)
+        combine(2, n)
+
+    loop(0, 2, first_far)
     loop(0, 4, partner_far)
-    wait_for(xin, pair_recv.at[2])
-    loop(0, 4, give_back_near)
-    loop(2, 4, lambda n: combine(2, n))
+
+    def last_far(n):
+        issue(n + 7)
+        combine(2, n)
+
+    loop(2, 4, last_far)
 
     loop(0, 3, own_far)
 
@@ -531,7 +555,6 @@
         sent(1, -3, -2, 3, 4)
         wait_for(tok.at[0, 0, 0], c_send.at[1, 1])
 
-    wait_for(xin, pair_send.at[2])
 
     def sent_groups(i):
         wait_for(tok.at[0, 0, 0], c_send.at[i % 2, i // 2])
@@ -545,10 +568,12 @@
         at = chunk(n)
         for i in (2, 3):
             wait_for(parts.at[i, pl.ds(0, SIDE - 1), :, at], b_send.at[i, n])
+        wait_for(xin.at[:, :, at], h_send.at[n])
 
     loop(0, D // CHUNK, sent_parts)
 
     def last_steps(n):
+        issue(n + 11)
         combine(0, n)
         own_near(n)
 
@@ -557,6 +582,17 @@
             own_far(3)
 
     loop(0, 4, last_steps)
+
+    def sent_chunks(n):
+        at = chunk(n)
+        for i in (0, 2, 3):
+            wait_for(mixed.at[i, 0, :, :, at], m_send.at[i, n])
+        wait_for(parts.at[0, pl.ds(0, SIDE - 1), :, at], b_send.at[0, n])
+        for way in range(4):
+            wait_for(zred.at[0, 0, :, at], q_send.at[way, n])
+        wait_for(zred.at[3, :, :, at], f_send.at[n])
+
+    loop(0, D // CHUNK, sent_chunks)
 
     def finish(n):
         at = chunk(n)
@@ -568,18 +604,11 @@
 
     loop(0, 4, finish)
 
-    def sent_chunks(n):
-        at = chunk(n)
-        for i in (0, 2, 3):
-            wait_for(mixed.at[i, 0, :, :, at], m_send.at[i, n])
-        wait_for(parts.at[0, pl.ds(0, SIDE - 1), :, at], b_send.at[0, n])
+    def sent_near(n):
         for way in range(3):
-            wait_for(zred.at[0, 0, :, at], nq_send.at[way, n])
-        for way in range(4):
-            wait_for(zred.at[0, 0, :, at], q_send.at[way, n])
-        wait_for(zred.at[3, :, :, at], f_send.at[n])
-
-    loop(0, D // CHUNK, sent_chunks)
+            wait_for(zred.at[0, 0, :, chunk(n)], nq_send.at[way, n])
+
+    loop(0, D // CHUNK, sent_near)
 
 
 def per_device(
@@ -623,7 +652,7 @@
             dma((6,)), dma((2, 4)), dma((2, 4)), dma((4,)), dma((4,)), dma((2,)), dma((2,)),
             dma((4,)), dma((4,)), dma((2, 8)), dma((2, 8)), dma((2, 2)), dma((2, 2)),
             dma((4,)), dma((4,)), dma((4, 4)), dma((4, 4)), dma((4, 4)), dma((4, 4)),
-            dma((4, 4)), dma((4,)), dma((4,)), dma((4,)), dma((3, 4)), dma((4,)),
+            dma((4, 4)), dma((4,)), dma((4,)), dma((4,)), dma((4,)), dma((4,)), dma((3, 4)), dma((4,)),
         ],
         compiler_params=pltpu.CompilerParams(
             collective_id=0, has_side_effects=True, vmem_limit_bytes=60 * 1024 * 1024

time: 137 us -> 137 us (level)
  no operation moved by 1% of the time
where the time goes in v7:
time: 137 us
  Pallas kernels  134 us (98%)
  local copies, waits for them, and re-layouts  1.68 us (1%)
    pallas_call x1, Pallas kernels, per_device(): pl.pallas_call(kernel, out_shape=jax.ShapeDtypeStruct((2, HERE, D), BF16)...  134 us

profile of v7, /device:TPU:1, one launch (start us, length us, event | category | flops | bytes accessed | tf_op | source)
XLA Modules:
  0.0 136.7 jit_solution(12148024745257393141)
XLA Ops:
  0.6 134.4 %shard_map.113 = bf16[2,32,2048]{2,1,0:T(8,128)(2,1)} custom-call(bf16[32,2048]{1,0:T(8,128)(2,1)} %bitcast.16, bf16[32,6144]{1,0:T(8,128)(2,1)} %bitcast.14, bf16[32,6144]{1,0:T(8,128)(2,1)} %bitcast.15, f32[1,2048]{1,0:T(1,128)} %bitcast.17, f32[1,2048]{1,0:T(1,128)} %bitcast.18, f32[1,2048]{1,0:T(1,128)} %bitcast.19, s32[6,1,32]{2,1,0:T(1,128)} %bitcast.20, ...), custom_call_target="tpu_custom_call" | custom-call | tf_op jit(solution)/shard_map/pallas_call | solution.py:633
  135.0 1.7 %fusion = (bf16[1,32,2048]{2,1,0:T(8,128)(2,1)}, bf16[1,32,2048]{2,1,0:T(8,128)(2,1)}) fusion(bf16[2,32,2048]{2,1,0:T(8,128)(2,1)} %shard_map.113), kind=kLoop, calls=%fused_computation | loop fusion | bytes 524288 | tf_op jit(solution)/shard_map/slice | solution.py:672
